TPU v7x, 512 devices: a whole 4x8x8 slice. The times are simulated.
512 devices in a mesh: along: 64 (over y_lo, z, core), cross: 8 (over x, y_hi).
Axes of the slice: x: 4, y: 8 (y_hi: 2, y_lo: 4; y = y_hi * 4 + y_lo), z: 8, core: 2. Of those that a mesh axis runs over, the one named last changes fastest.
Arguments:
- surface: float32 [8192, 2048], P('along', 'cross'), may hold values from -6 to 6
- along_speed: float32 [8192, 2048], P('along', 'cross'), may hold values from -3 to 3
- cross_speed: float32 [8192, 2048], P('along', 'cross'), may hold values from -3 to 3
- water_depth: float32 [8192, 2048], P('along', 'cross'), may hold values from 0.5 to 2
- wet_mask: int32 [8192, 2048], P('along', 'cross'), may hold values 0 or 1
- ship_cells: int32 [2, 8], replicated, may hold values from 0 to 16777215
- ship_pressure: float32 [8], replicated, may hold values from 1 to 4
Outputs:
- surface_out: float32 [8192, 2048], P('along', 'cross')
- along_out: float32 [8192, 2048], P('along', 'cross')
- cross_out: float32 [8192, 2048], P('along', 'cross')
- current_along: float32 [8192, 2048], P('along', 'cross')
- current_cross: float32 [8192, 2048], P('along', 'cross')
Inputs may be any that keep to these rules, and one draw needn't show every extreme that they name: `ship_cells`: each entry is a cell index row * 2048 + column.
All inputs are finite; a program needn't handle non-finite values. No bound on the sum of `wet_mask` on one device may be relied on, other than what follows from the above.
Results may differ from a plain program's by a relative error of at most 0.0003.
Values sent between devices are 32-bit elements; how exact they have to be, the bound alone decides.
A program may use at most 64 MiB of HBM per device.

v0:
```python
import jax
import jax.numpy as jnp
from jax import lax
from jax.sharding import PartitionSpec as P

STEPS = 2
CIRC = 3


CONTINUITY = 0.25
MOMENTUM = 0.3
POTENTIAL = 0.5
CIRC_LEVEL = 0.2
CIRC_FORCE = 0.3
FRICTION = 0.1
VISCOSITY = 0.1


def padded_2(cells, sides, width):
    for axis, dim in sides:
        count = lax.axis_size(axis)
        ends = count - 1
        head = lax.slice_in_dim(cells, 0, width, axis=dim)
        tail = lax.slice_in_dim(cells, cells.shape[dim] - width, cells.shape[dim], axis=dim)
        cells = jnp.concatenate(
            [
                lax.ppermute(tail, axis, [(i, (i + 1) % count) for i in range(ends)]),
                cells,
                lax.ppermute(head, axis, [((i + 1) % count, i) for i in range(ends)]),
            ],
            axis=dim,
        )
    return cells


def diff_rows(values):
    return 0.5 * (values[..., 2:, 1:-1] - values[..., :-2, 1:-1])


def diff_cols(values):
    return 0.5 * (values[..., 1:-1, 2:] - values[..., 1:-1, :-2])


def laplace(values):
    return (
        values[..., 2:, 1:-1]
        + values[..., :-2, 1:-1]
        + values[..., 1:-1, 2:]
        + values[..., 1:-1, :-2]
        - 4.0 * values[..., 1:-1, 1:-1]
    )


def interior(values, layers):
    return values[..., layers : values.shape[-2] - layers, layers : values.shape[-1] - layers]


def advance_waves(surface, along_speed, cross_speed, water_depth, wet_share, forcing):
    mass_flux = diff_rows(water_depth * along_speed) + diff_cols(water_depth * cross_speed)
    raised = interior(wet_share, 1) * (
        interior(surface, 1) - CONTINUITY * mass_flux + interior(forcing, 1)
    )
    curvature = laplace(raised)
    depth_inner = interior(water_depth, 3)
    dispersion = depth_inner * depth_inner / 3.0
    push_along = interior(diff_rows(raised), 1) + dispersion * diff_rows(curvature)
    push_cross = interior(diff_cols(raised), 1) + dispersion * diff_cols(curvature)
    wet_inner = interior(wet_share, 3)
    return (
        interior(raised, 2),
        wet_inner * (interior(along_speed, 3) - MOMENTUM * push_along),
        wet_inner * (interior(cross_speed, 3) - MOMENTUM * push_cross),
    )


def radiation(water_depth, surface, along_speed, cross_speed):
    potential_part = POTENTIAL * surface * surface
    return jnp.stack(
        [
            water_depth * along_speed * along_speed + potential_part,
            water_depth * along_speed * cross_speed,
            water_depth * cross_speed * cross_speed + potential_part,
        ]
    )


def restrict(values):
    leading = values.shape[:-2]
    fine_rows = values.shape[-2]
    fine_cols = values.shape[-1]
    blocks = values.reshape(leading + (fine_rows // 4, 4, fine_cols // 4, 4))
    return jnp.mean(blocks, axis=(-3, -1))


def circulate(coarse, rim):
    depth_coarse = coarse[3]
    wet_coarse = coarse[4]
    stress_wide = rim(coarse[0:3])
    force_along = -(diff_rows(stress_wide[0]) + diff_cols(stress_wide[1])) / depth_coarse
    force_cross = -(diff_rows(stress_wide[1]) + diff_cols(stress_wide[2])) / depth_coarse
    elevation = jnp.zeros_like(depth_coarse)
    flow_along = jnp.zeros_like(depth_coarse)
    flow_cross = jnp.zeros_like(depth_coarse)
    for circ_sweep in range(CIRC):
        moving = rim(
            jnp.stack(
                [depth_coarse * flow_along, depth_coarse * flow_cross, flow_along, flow_cross]
            )
        )
        elevation = elevation - CIRC_LEVEL * (diff_rows(moving[0]) + diff_cols(moving[1]))
        surface_slope = rim(elevation[None])[0]
        new_along = wet_coarse * (
            flow_along
            + CIRC_FORCE * (force_along - diff_rows(surface_slope))
            - FRICTION * flow_along / depth_coarse
            + VISCOSITY * laplace(moving[2])
        )
        new_cross = wet_coarse * (
            flow_cross
            + CIRC_FORCE * (force_cross - diff_cols(surface_slope))
            - FRICTION * flow_cross / depth_coarse
            + VISCOSITY * laplace(moving[3])
        )
        flow_along = new_along
        flow_cross = new_cross
    return jnp.stack([flow_along, flow_cross])


def refine_dim(values, along_dim):
    coarse_count = values.shape[along_dim] - 2
    center = lax.slice_in_dim(values, 1, coarse_count + 1, axis=along_dim)
    previous = lax.slice_in_dim(values, 0, coarse_count, axis=along_dim)
    following = lax.slice_in_dim(values, 2, coarse_count + 2, axis=along_dim)
    pieces = jnp.stack(
        [
            0.625 * center + 0.375 * previous,
            0.875 * center + 0.125 * previous,
            0.875 * center + 0.125 * following,
            0.625 * center + 0.375 * following,
        ],
        axis=along_dim + 1,
    )
    new_shape = list(center.shape)
    new_shape[along_dim] = 4 * coarse_count
    return pieces.reshape(tuple(new_shape))


def refine(values):
    return refine_dim(refine_dim(values, 1), 2)


def ship_forcing(cells, pressure, first_row, first_col, count_rows, count_cols, total_cols):
    ship_rows = cells // total_cols
    ship_cols = cells % total_cols
    row_hits = (
        ship_rows[:, None] == first_row + jnp.arange(count_rows, dtype=jnp.int32)[None, :]
    ).astype(jnp.float32)
    row_hits = row_hits * pressure[:, None]
    col_hits = (
        ship_cols[:, None] == first_col + jnp.arange(count_cols, dtype=jnp.int32)[None, :]
    ).astype(jnp.float32)
    return jnp.dot(
        row_hits.T, col_hits, precision=lax.Precision.HIGHEST, preferred_element_type=jnp.float32
    )


def slab_rim(values):
    padded = padded_2(values, ((("along", "cross"), 1),), 1)
    return jnp.pad(padded, ((0, 0), (0, 0), (1, 1)))


def per_device(surface, along_speed, cross_speed, water_depth, wet_mask, ship_cells, ship_pressure):
    tile_rows = surface.shape[0]
    tile_cols = surface.shape[1]
    total_cols = tile_cols * lax.axis_size("cross")
    first_row = lax.axis_index("along") * tile_rows
    first_col = lax.axis_index("cross") * tile_cols
    wet_share = wet_mask.astype(jnp.float32)
    stress = jnp.zeros((3, tile_rows, tile_cols), jnp.float32)
    level_now = surface
    along_now = along_speed
    cross_now = cross_speed
    for wave_section in range(STEPS):
        widened = padded_2(
            jnp.stack([level_now, along_now, cross_now, water_depth, wet_share]),
            (("along", 1), ("cross", 2)),
            3,
        )
        forcing = ship_forcing(
            ship_cells[wave_section],
            ship_pressure,
            first_row - 3,
            first_col - 3,
            tile_rows + 6,
            tile_cols + 6,
            total_cols,
        )
        level_now, along_now, cross_now = advance_waves(
            widened[0], widened[1], widened[2], widened[3], widened[4], forcing
        )
        stress = stress + radiation(water_depth, level_now, along_now, cross_now)
    stress = stress / STEPS
    fields = jnp.concatenate([stress, jnp.stack([water_depth, wet_share])], axis=0)
    slab_fields = lax.all_to_all(restrict(fields), "cross", split_axis=1, concat_axis=2, tiled=True)
    slab_flows = circulate(slab_fields, slab_rim)
    currents = lax.all_to_all(slab_flows, "cross", split_axis=2, concat_axis=1, tiled=True)
    widened_currents = padded_2(currents, (("along", 1), ("cross", 2)), 1)
    fine_currents = refine(widened_currents)
    return (
        level_now,
        along_now,
        cross_now,
        fine_currents[0] * wet_share,
        fine_currents[1] * wet_share,
    )


def solution(mesh):
    return jax.shard_map(
        per_device,
        mesh=mesh,
        in_specs=(
            P("along", "cross"),
            P("along", "cross"),
            P("along", "cross"),
            P("along", "cross"),
            P("along", "cross"),
            P(),
            P(),
        ),
        out_specs=(
            P("along", "cross"),
            P("along", "cross"),
            P("along", "cross"),
            P("along", "cross"),
            P("along", "cross"),
        ),
        check_vma=False,
    )
```

profile of v0, /device:TPU:233, one launch (start us, length us, event | category | flops | bytes accessed | tf_op | source)
XLA Modules:
  0.0 319.0 jit_solution(12906582846224445992)
XLA Ops:
  0.6 0.9 bitcast_dynamic-update-slice_fusion.9
  1.5 0.9 bitcast_dynamic-update-slice_fusion.8
  2.5 0.9 bitcast_dynamic-update-slice_fusion.7
  3.4 0.9 bitcast_dynamic-update-slice_fusion.6
  4.3 0.9 bitcast_dynamic-update-slice_fusion.4
  5.2 5.8 %collective-permute-start = (f32[5,3,256]{2,1,0:T(4,128)S(1)}, f32[5,3,256]{2,1,0:T(4,128)S(1)}, u32[]{:S(2)}, u32[]{:S(2)}) collective-permute-start(f32[5,3,256]{2,1,0:T(4,128)S(1)} %get-tuple-element.48), channel_id=1, source_target_pairs={{0,8},{8,16},{16,24},{24,32},{32,40},{40,48},{48,56},{56,64},{64,7... | collective-permute-start | bytes 46088 | tf_op jit(solution)/shard_map/ppermute | solution.py:27
  11.0 1.9 collective-permute-start.1
  13.0 0.8 and_select_fusion.1
  13.8 3.6 %collective-permute-done.1 = f32[5,3,256]{2,1,0:T(4,128)S(1)} collective-permute-done((f32[5,3,256]{2,1,0:T(4,128)S(1)}, f32[5,3,256]{2,1,0:T(4,128)S(1)}, u32[]{:S(2)}, u32[]{:S(2)}) %collective-permute-start.1) | collective-permute-done | bytes 15392 | tf_op jit(solution)/shard_map/ppermute | solution.py:29
  17.6 3.6 %collective-permute-start.2 = (f32[5,134,3]{2,1,0:T(8,128)S(1)}, f32[5,134,3]{2,1,0:T(8,128)S(1)}, u32[]{:S(2)}, u32[]{:S(2)}) collective-permute-start(f32[5,134,3]{2,1,0:T(8,128)S(1)} %get-tuple-element.44), channel_id=1, source_target_pairs={{0,1},{1,2},{2,3},{3,4},{4,5},{5,6},{6,7},{8,9},{9,10},{10,11},{11... | collective-permute-start | bytes 24128 | tf_op jit(solution)/shard_map/ppermute | solution.py:27
  21.1 5.6 %collective-permute-start.3 = (f32[5,134,3]{2,1,0:T(8,128)S(1)}, f32[5,134,3]{2,1,0:T(8,128)S(1)}, u32[]{:S(2)}, u32[]{:S(2)}) collective-permute-start(f32[5,134,3]{2,1,0:T(8,128)S(1)} %get-tuple-element.45), channel_id=1, source_target_pairs={{1,0},{2,1},{3,2},{4,3},{5,4},{6,5},{7,6},{9,8},{10,9},{11,10},{12... | collective-permute-start | bytes 24128 | tf_op jit(solution)/shard_map/ppermute | solution.py:29
  26.9 11.3 %collective-permute-done.2 = f32[5,134,3]{2,1,0:T(8,128)S(1)} collective-permute-done((f32[5,134,3]{2,1,0:T(8,128)S(1)}, f32[5,134,3]{2,1,0:T(8,128)S(1)}, u32[]{:S(2)}, u32[]{:S(2)}) %collective-permute-start.2) | collective-permute-done | bytes 8072 | tf_op jit(solution)/shard_map/ppermute | solution.py:27
  38.2 15.6 %collective-permute-done.3 = f32[5,134,3]{2,1,0:T(8,128)S(1)} collective-permute-done((f32[5,134,3]{2,1,0:T(8,128)S(1)}, f32[5,134,3]{2,1,0:T(8,128)S(1)}, u32[]{:S(2)}, u32[]{:S(2)}) %collective-permute-start.3) | collective-permute-done | bytes 8072 | tf_op jit(solution)/shard_map/ppermute | solution.py:29
  56.2 5.2 %collective-permute-start.4 = (f32[5,3,256]{2,1,0:T(4,128)S(1)}, f32[5,3,256]{2,1,0:T(4,128)S(1)}, u32[]{:S(2)}, u32[]{:S(2)}) collective-permute-start(f32[5,3,256]{2,1,0:T(4,128)S(1)} %get-tuple-element.46), channel_id=1, source_target_pairs={{0,8},{8,16},{16,24},{24,32},{32,40},{40,48},{48,56},{56,64},{64,7... | collective-permute-start | bytes 46088 | tf_op jit(solution)/shard_map/ppermute | solution.py:27
  61.4 1.9 collective-permute-start.5
  63.3 4.4 %collective-permute-done.5 = f32[5,3,256]{2,1,0:T(4,128)S(1)} collective-permute-done((f32[5,3,256]{2,1,0:T(4,128)S(1)}, f32[5,3,256]{2,1,0:T(4,128)S(1)}, u32[]{:S(2)}, u32[]{:S(2)}) %collective-permute-start.5) | collective-permute-done | bytes 15392 | tf_op jit(solution)/shard_map/ppermute | solution.py:29
  67.8 0.9 fusion.153
  68.7 3.6 %collective-permute-start.6 = (f32[5,134,3]{2,1,0:T(8,128)}, f32[5,134,3]{2,1,0:T(8,128)S(1)}, u32[]{:S(2)}, u32[]{:S(2)}) collective-permute-start(f32[5,134,3]{2,1,0:T(8,128)} %get-tuple-element.42), channel_id=1, source_target_pairs={{0,1},{1,2},{2,3},{3,4},{4,5},{5,6},{6,7},{8,9},{9,10},{10,11},{11... | collective-permute-start | bytes 24128 | tf_op jit(solution)/shard_map/ppermute | solution.py:27
  72.3 5.8 %collective-permute-start.7 = (f32[5,134,3]{2,1,0:T(8,128)}, f32[5,134,3]{2,1,0:T(8,128)S(1)}, u32[]{:S(2)}, u32[]{:S(2)}) collective-permute-start(f32[5,134,3]{2,1,0:T(8,128)} %get-tuple-element.43), channel_id=1, source_target_pairs={{1,0},{2,1},{3,2},{4,3},{5,4},{6,5},{7,6},{9,8},{10,9},{11,10},{12... | collective-permute-start | bytes 24128 | tf_op jit(solution)/shard_map/ppermute | solution.py:29
  78.1 5.7 %concatenate.53 = f32[1,32,4,64,4]{4,3,2,1,0:T(8,128)} reshape(f32[128,256]{1,0:T(8,128)S(1)} %copy-done) | data formatting | bytes 262144 | tf_op jit(solution)/shard_map/concatenate | solution.py:203
  83.8 5.7 %concatenate.54 = f32[1,32,4,64,4]{4,3,2,1,0:T(8,128)} reshape(f32[128,256]{1,0:T(8,128)S(1)} %convert_element_type.17) | data formatting | bytes 262144 | tf_op jit(solution)/shard_map/concatenate | solution.py:203
  89.5 3.0 copy.93
  92.6 3.0 copy.92
  95.6 5.7 %stack.146 = f32[1,32,4,64,4]{4,3,2,1,0:T(8,128)} reshape(f32[128,256]{1,0:T(8,128)S(1)} %get-tuple-element.22) | data formatting | bytes 262144 | tf_op jit(solution)/shard_map/stack | solution.py:78
  101.3 3.0 copy.87
  104.3 5.7 %stack.145 = f32[1,32,4,64,4]{4,3,2,1,0:T(8,128)} reshape(f32[128,256]{1,0:T(8,128)S(1)} %get-tuple-element.20) | data formatting | bytes 262144 | tf_op jit(solution)/shard_map/stack | solution.py:78
  110.0 3.0 copy.86
  115.3 5.7 %stack.147 = f32[1,32,4,64,4]{4,3,2,1,0:T(8,128)} reshape(f32[128,256]{1,0:T(8,128)S(1)} %get-tuple-element.69) | data formatting | bytes 262144 | tf_op jit(solution)/shard_map/stack | solution.py:78
  121.0 3.0 copy.88
  124.0 5.7 %stack.151 = f32[1,32,4,64,4]{4,3,2,1,0:T(8,128)} reshape(f32[128,256]{1,0:T(8,128)S(1)} %get-tuple-element.68) | data formatting | bytes 262144 | tf_op jit(solution)/shard_map/stack | solution.py:78
  129.7 3.0 copy.91
  132.8 5.9 %stack.150 = f32[1,32,4,64,4]{4,3,2,1,0:T(8,128)} reshape(f32[128,256]{1,0:T(8,128)S(1)} %get-tuple-element.18) | data formatting | bytes 262144 | tf_op jit(solution)/shard_map/stack | solution.py:78
  138.7 3.0 copy.90
  141.7 5.7 %stack.149 = f32[1,32,4,64,4]{4,3,2,1,0:T(8,128)} reshape(f32[128,256]{1,0:T(8,128)S(1)} %get-tuple-element.15) | data formatting | bytes 262144 | tf_op jit(solution)/shard_map/stack | solution.py:78
  147.4 3.0 copy.89
  150.9 12.7 %all_to_all.33 = f32[8,1,1280]{2,1,0:T(1,128)S(1)} all-to-all(f32[8,1,1280]{2,1,0:T(1,128)S(1)} %reshape.163), channel_id=1, replica_groups=mesh['along'=64,'cross'=8] {'cross'}, dimensions={0} | all-to-all | bytes 81920 | tf_op jit(solution)/shard_map/all_to_all | solution.py:204
  165.1 6.9 %collective-permute-start.8 = (f32[3,1,512]{2,1,0:T(1,128)S(1)}, f32[3,1,512]{2,1,0:T(1,128)S(1)}, u32[]{:S(2)}, u32[]{:S(2)}) collective-permute-start(f32[3,1,512]{2,1,0:T(1,128)S(1)} %get-tuple-element.100), channel_id=1, source_target_pairs={{0,1},{1,2},{2,3},{3,4},{4,5},{5,6},{6,7},{7,8},{8,9},{9,10},{10,1... | collective-permute-start | bytes 18440 | tf_op jit(solution)/shard_map/ppermute | solution.py:27
  172.0 2.3 collective-permute-start.9
  174.4 7.8 %collective-permute-start.10 = (f32[4,1,512]{2,1,0:T(1,128)S(1)}, f32[4,1,512]{2,1,0:T(1,128)S(1)}, u32[]{:S(2)}, u32[]{:S(2)}) collective-permute-start(f32[4,1,512]{2,1,0:T(1,128)S(1)} %get-tuple-element.102), channel_id=1, source_target_pairs={{0,1},{1,2},{2,3},{3,4},{4,5},{5,6},{6,7},{7,8},{8,9},{9,10},{10,1... | collective-permute-start | bytes 24584 | tf_op jit(solution)/shard_map/ppermute | solution.py:27
  182.2 3.4 %collective-permute-start.11 = (f32[4,1,512]{2,1,0:T(1,128)S(1)}, f32[4,1,512]{2,1,0:T(1,128)S(1)}, u32[]{:S(2)}, u32[]{:S(2)}) collective-permute-start(f32[4,1,512]{2,1,0:T(1,128)S(1)} %get-tuple-element.103), channel_id=1, source_target_pairs={{1,0},{2,1},{3,2},{4,3},{5,4},{6,5},{7,6},{8,7},{9,8},{10,9},{11,1... | collective-permute-start | bytes 24584 | tf_op jit(solution)/shard_map/ppermute | solution.py:29
  185.9 5.8 %collective-permute-done.11 = f32[4,1,512]{2,1,0:T(1,128)S(1)} collective-permute-done((f32[4,1,512]{2,1,0:T(1,128)S(1)}, f32[4,1,512]{2,1,0:T(1,128)S(1)}, u32[]{:S(2)}, u32[]{:S(2)}) %collective-permute-start.11) | collective-permute-done | bytes 8224 | tf_op jit(solution)/shard_map/ppermute | solution.py:29
  192.0 1.9 collective-permute-start.12
  193.9 7.3 %collective-permute-start.13 = (f32[1,1,512]{2,1,0:T(1,128)S(1)}, f32[1,1,512]{2,1,0:T(1,128)S(1)}, u32[]{:S(2)}, u32[]{:S(2)}) collective-permute-start(f32[1,1,512]{2,1,0:T(1,128)S(1)} %get-tuple-element.109), channel_id=1, source_target_pairs={{1,0},{2,1},{3,2},{4,3},{5,4},{6,5},{7,6},{8,7},{9,8},{10,9},{11,1... | collective-permute-start | bytes 6152 | tf_op jit(solution)/shard_map/ppermute | solution.py:29
  201.2 1.8 collective-permute-done.13
  203.4 6.4 %collective-permute-start.14 = (f32[4,1,512]{2,1,0:T(1,128)S(1)}, f32[4,1,512]{2,1,0:T(1,128)S(1)}, u32[]{:S(2)}, u32[]{:S(2)}) collective-permute-start(f32[4,1,512]{2,1,0:T(1,128)S(1)} %get-tuple-element.98), channel_id=1, source_target_pairs={{0,1},{1,2},{2,3},{3,4},{4,5},{5,6},{6,7},{7,8},{8,9},{9,10},{10,1... | collective-permute-start | bytes 24584 | tf_op jit(solution)/shard_map/ppermute | solution.py:27
  209.8 2.8 collective-permute-start.15
  212.6 6.4 %collective-permute-done.15 = f32[4,1,512]{2,1,0:T(1,128)S(1)} collective-permute-done((f32[4,1,512]{2,1,0:T(1,128)S(1)}, f32[4,1,512]{2,1,0:T(1,128)S(1)}, u32[]{:S(2)}, u32[]{:S(2)}) %collective-permute-start.15) | collective-permute-done | bytes 8224 | tf_op jit(solution)/shard_map/ppermute | solution.py:29
  219.3 2.4 collective-permute-start.16
  221.7 6.8 %collective-permute-start.17 = (f32[1,1,512]{2,1,0:T(1,128)S(1)}, f32[1,1,512]{2,1,0:T(1,128)S(1)}, u32[]{:S(2)}, u32[]{:S(2)}) collective-permute-start(f32[1,1,512]{2,1,0:T(1,128)S(1)} %get-tuple-element.107), channel_id=1, source_target_pairs={{1,0},{2,1},{3,2},{4,3},{5,4},{6,5},{7,6},{8,7},{9,8},{10,9},{11,1... | collective-permute-start | bytes 6152 | tf_op jit(solution)/shard_map/ppermute | solution.py:29
  228.5 6.0 %collective-permute-done.17 = f32[1,1,512]{2,1,0:T(1,128)S(1)} collective-permute-done((f32[1,1,512]{2,1,0:T(1,128)S(1)}, f32[1,1,512]{2,1,0:T(1,128)S(1)}, u32[]{:S(2)}, u32[]{:S(2)}) %collective-permute-start.17) | collective-permute-done | bytes 2080 | tf_op jit(solution)/shard_map/ppermute | solution.py:29
  234.8 7.5 %collective-permute-start.18 = (f32[4,1,512]{2,1,0:T(1,128)S(1)}, f32[4,1,512]{2,1,0:T(1,128)S(1)}, u32[]{:S(2)}, u32[]{:S(2)}) collective-permute-start(f32[4,1,512]{2,1,0:T(1,128)S(1)} %get-tuple-element.96), channel_id=1, source_target_pairs={{0,1},{1,2},{2,3},{3,4},{4,5},{5,6},{6,7},{7,8},{8,9},{9,10},{10,1... | collective-permute-start | bytes 24584 | tf_op jit(solution)/shard_map/ppermute | solution.py:27
  242.3 1.9 collective-permute-start.19
  244.2 7.3 %collective-permute-done.19 = f32[4,1,512]{2,1,0:T(1,128)S(1)} collective-permute-done((f32[4,1,512]{2,1,0:T(1,128)S(1)}, f32[4,1,512]{2,1,0:T(1,128)S(1)}, u32[]{:S(2)}, u32[]{:S(2)}) %collective-permute-start.19) | collective-permute-done | bytes 8224 | tf_op jit(solution)/shard_map/ppermute | solution.py:29
  251.7 7.1 %collective-permute-start.20 = (f32[1,1,512]{2,1,0:T(1,128)S(1)}, f32[1,1,512]{2,1,0:T(1,128)S(1)}, u32[]{:S(2)}, u32[]{:S(2)}) collective-permute-start(f32[1,1,512]{2,1,0:T(1,128)S(1)} %get-tuple-element.104), channel_id=1, source_target_pairs={{0,1},{1,2},{2,3},{3,4},{4,5},{5,6},{6,7},{7,8},{8,9},{9,10},{10,1... | collective-permute-start | bytes 6152 | tf_op jit(solution)/shard_map/ppermute | solution.py:27
  258.8 2.1 collective-permute-start.21
  260.9 7.0 %collective-permute-done.21 = f32[1,1,512]{2,1,0:T(1,128)S(1)} collective-permute-done((f32[1,1,512]{2,1,0:T(1,128)S(1)}, f32[1,1,512]{2,1,0:T(1,128)S(1)}, u32[]{:S(2)}, u32[]{:S(2)}) %collective-permute-start.21) | collective-permute-done | bytes 2080 | tf_op jit(solution)/shard_map/ppermute | solution.py:29
  269.3 21.7 %all_to_all.34 = f32[8,1,512]{2,1,0:T(1,128)S(1)} all-to-all(f32[8,1,512]{2,1,0:T(1,128)S(1)} %reshape.165), channel_id=1, replica_groups=mesh['along'=64,'cross'=8] {'cross'}, dimensions={0} | all-to-all | bytes 32768 | tf_op jit(solution)/shard_map/all_to_all | solution.py:206
  291.6 0.8 reshape.166
  292.7 1.9 collective-permute-start.22
  294.6 2.4 collective-permute-start.23
  297.1 3.7 %collective-permute-done.23 = f32[2,1,64]{2,1,0:T(1,128)S(1)} collective-permute-done((f32[2,1,64]{2,1,0:T(1,128)S(1)}, f32[2,1,64]{2,1,0:T(1,128)S(1)}, u32[]{:S(2)}, u32[]{:S(2)}) %collective-permute-start.23) | collective-permute-done | bytes 544 | tf_op jit(solution)/shard_map/ppermute | solution.py:29
  300.8 6.9 %collective-permute-start.24 = (f32[2,34,1]{2,1,0:T(8,128)S(1)}, f32[2,34,1]{2,1,0:T(8,128)S(1)}, u32[]{:S(2)}, u32[]{:S(2)}) collective-permute-start(f32[2,34,1]{2,1,0:T(8,128)S(1)} %get-tuple-element.92), channel_id=1, source_target_pairs={{0,1},{1,2},{2,3},{3,4},{4,5},{5,6},{6,7},{8,9},{9,10},{10,11},{11... | collective-permute-start | bytes 824 | tf_op jit(solution)/shard_map/ppermute | solution.py:27
  307.8 2.2 collective-permute-start.25
  310.0 7.3 %collective-permute-done.25 = f32[2,34,1]{2,1,0:T(8,128)S(1)} collective-permute-done((f32[2,34,1]{2,1,0:T(8,128)S(1)}, f32[2,34,1]{2,1,0:T(8,128)S(1)}, u32[]{:S(2)}, u32[]{:S(2)}) %collective-permute-start.25) | collective-permute-done | bytes 304 | tf_op jit(solution)/shard_map/ppermute | solution.py:29
  (122 shorter events, 12.5 us)
Async XLA Ops:
  5.2 8.5 %collective-permute-start = (f32[5,3,256]{2,1,0:T(4,128)S(1)}, f32[5,3,256]{2,1,0:T(4,128)S(1)}, u32[]{:S(2)}, u32[]{:S(2)}) collective-permute-start(f32[5,3,256]{2,1,0:T(4,128)S(1)} %get-tuple-element.48), channel_id=1, source_target_pairs={{0,8},{8,16},{16,24},{24,32},{32,40},{40,48},{48,56},{56,64},{64,7... | collective-permute-start | bytes 46088 | tf_op jit(solution)/shard_map/ppermute | solution.py:27
  11.0 6.3 %collective-permute-start.1 = (f32[5,3,256]{2,1,0:T(4,128)S(1)}, f32[5,3,256]{2,1,0:T(4,128)S(1)}, u32[]{:S(2)}, u32[]{:S(2)}) collective-permute-start(f32[5,3,256]{2,1,0:T(4,128)S(1)} %get-tuple-element.49), channel_id=1, source_target_pairs={{8,0},{16,8},{24,16},{32,24},{40,32},{48,40},{56,48},{64,56},{72,6... | collective-permute-start | bytes 46088 | tf_op jit(solution)/shard_map/ppermute | solution.py:29
  13.7 40.7 %copy-start.5 = (f32[8]{0:T(128)S(1)}, f32[8]{0:T(128)}, u32[]{:S(2)}) copy-start(f32[8]{0:T(128)} %param.13) | copy-start | bytes 100
  17.6 20.7 %collective-permute-start.2 = (f32[5,134,3]{2,1,0:T(8,128)S(1)}, f32[5,134,3]{2,1,0:T(8,128)S(1)}, u32[]{:S(2)}, u32[]{:S(2)}) collective-permute-start(f32[5,134,3]{2,1,0:T(8,128)S(1)} %get-tuple-element.44), channel_id=1, source_target_pairs={{0,1},{1,2},{2,3},{3,4},{4,5},{5,6},{6,7},{8,9},{9,10},{10,11},{11... | collective-permute-start | bytes 24128 | tf_op jit(solution)/shard_map/ppermute | solution.py:27
  21.1 32.7 %collective-permute-start.3 = (f32[5,134,3]{2,1,0:T(8,128)S(1)}, f32[5,134,3]{2,1,0:T(8,128)S(1)}, u32[]{:S(2)}, u32[]{:S(2)}) collective-permute-start(f32[5,134,3]{2,1,0:T(8,128)S(1)} %get-tuple-element.45), channel_id=1, source_target_pairs={{1,0},{2,1},{3,2},{4,3},{5,4},{6,5},{7,6},{9,8},{10,9},{11,10},{12... | collective-permute-start | bytes 24128 | tf_op jit(solution)/shard_map/ppermute | solution.py:29
  26.9 28.4 %copy-start = (f32[128,256]{1,0:T(8,128)S(1)}, f32[128,256]{1,0:T(8,128)}, u32[]{:S(2)}) copy-start(f32[128,256]{1,0:T(8,128)} %param.10) | copy-start | bytes 393220
  54.4 1.7 copy-start.1
  56.2 7.2 %collective-permute-start.4 = (f32[5,3,256]{2,1,0:T(4,128)S(1)}, f32[5,3,256]{2,1,0:T(4,128)S(1)}, u32[]{:S(2)}, u32[]{:S(2)}) collective-permute-start(f32[5,3,256]{2,1,0:T(4,128)S(1)} %get-tuple-element.46), channel_id=1, source_target_pairs={{0,8},{8,16},{16,24},{24,32},{32,40},{40,48},{48,56},{56,64},{64,7... | collective-permute-start | bytes 46088 | tf_op jit(solution)/shard_map/ppermute | solution.py:27
  61.4 6.3 %collective-permute-start.5 = (f32[5,3,256]{2,1,0:T(4,128)S(1)}, f32[5,3,256]{2,1,0:T(4,128)S(1)}, u32[]{:S(2)}, u32[]{:S(2)}) collective-permute-start(f32[5,3,256]{2,1,0:T(4,128)S(1)} %get-tuple-element.47), channel_id=1, source_target_pairs={{8,0},{16,8},{24,16},{32,24},{40,32},{48,40},{56,48},{64,56},{72,6... | collective-permute-start | bytes 46088 | tf_op jit(solution)/shard_map/ppermute | solution.py:29
  68.7 44.3 %collective-permute-start.6 = (f32[5,134,3]{2,1,0:T(8,128)}, f32[5,134,3]{2,1,0:T(8,128)S(1)}, u32[]{:S(2)}, u32[]{:S(2)}) collective-permute-start(f32[5,134,3]{2,1,0:T(8,128)} %get-tuple-element.42), channel_id=1, source_target_pairs={{0,1},{1,2},{2,3},{3,4},{4,5},{5,6},{6,7},{8,9},{9,10},{10,11},{11... | collective-permute-start | bytes 24128 | tf_op jit(solution)/shard_map/ppermute | solution.py:27
  72.3 40.7 %collective-permute-start.7 = (f32[5,134,3]{2,1,0:T(8,128)}, f32[5,134,3]{2,1,0:T(8,128)S(1)}, u32[]{:S(2)}, u32[]{:S(2)}) collective-permute-start(f32[5,134,3]{2,1,0:T(8,128)} %get-tuple-element.43), channel_id=1, source_target_pairs={{1,0},{2,1},{3,2},{4,3},{5,4},{6,5},{7,6},{9,8},{10,9},{11,10},{12... | collective-permute-start | bytes 24128 | tf_op jit(solution)/shard_map/ppermute | solution.py:29
  114.8 9.2 %copy-start.2 = (f32[128,256]{1,0:T(8,128)}, f32[128,256]{1,0:T(8,128)S(1)}, u32[]{:S(2)}) copy-start(f32[128,256]{1,0:T(8,128)S(1)} %get-tuple-element.17) | copy-start | bytes 393220
  114.9 9.2 %copy-start.3 = (f32[128,256]{1,0:T(8,128)}, f32[128,256]{1,0:T(8,128)S(1)}, u32[]{:S(2)}) copy-start(f32[128,256]{1,0:T(8,128)S(1)} %get-tuple-element.16) | copy-start | bytes 393220
  115.2 8.9 %copy-start.4 = (f32[128,256]{1,0:T(8,128)}, f32[128,256]{1,0:T(8,128)S(1)}, u32[]{:S(2)}) copy-start(f32[128,256]{1,0:T(8,128)S(1)} %get-tuple-element.19) | copy-start | bytes 393220
  165.1 20.7 %collective-permute-start.8 = (f32[3,1,512]{2,1,0:T(1,128)S(1)}, f32[3,1,512]{2,1,0:T(1,128)S(1)}, u32[]{:S(2)}, u32[]{:S(2)}) collective-permute-start(f32[3,1,512]{2,1,0:T(1,128)S(1)} %get-tuple-element.100), channel_id=1, source_target_pairs={{0,1},{1,2},{2,3},{3,4},{4,5},{5,6},{6,7},{7,8},{8,9},{9,10},{10,1... | collective-permute-start | bytes 18440 | tf_op jit(solution)/shard_map/ppermute | solution.py:27
  172.0 13.8 %collective-permute-start.9 = (f32[3,1,512]{2,1,0:T(1,128)S(1)}, f32[3,1,512]{2,1,0:T(1,128)S(1)}, u32[]{:S(2)}, u32[]{:S(2)}) collective-permute-start(f32[3,1,512]{2,1,0:T(1,128)S(1)} %get-tuple-element.101), channel_id=1, source_target_pairs={{1,0},{2,1},{3,2},{4,3},{5,4},{6,5},{7,6},{8,7},{9,8},{10,9},{11,1... | collective-permute-start | bytes 18440 | tf_op jit(solution)/shard_map/ppermute | solution.py:29
  174.4 11.5 %collective-permute-start.10 = (f32[4,1,512]{2,1,0:T(1,128)S(1)}, f32[4,1,512]{2,1,0:T(1,128)S(1)}, u32[]{:S(2)}, u32[]{:S(2)}) collective-permute-start(f32[4,1,512]{2,1,0:T(1,128)S(1)} %get-tuple-element.102), channel_id=1, source_target_pairs={{0,1},{1,2},{2,3},{3,4},{4,5},{5,6},{6,7},{7,8},{8,9},{9,10},{10,1... | collective-permute-start | bytes 24584 | tf_op jit(solution)/shard_map/ppermute | solution.py:27
  182.2 9.5 %collective-permute-start.11 = (f32[4,1,512]{2,1,0:T(1,128)S(1)}, f32[4,1,512]{2,1,0:T(1,128)S(1)}, u32[]{:S(2)}, u32[]{:S(2)}) collective-permute-start(f32[4,1,512]{2,1,0:T(1,128)S(1)} %get-tuple-element.103), channel_id=1, source_target_pairs={{1,0},{2,1},{3,2},{4,3},{5,4},{6,5},{7,6},{8,7},{9,8},{10,9},{11,1... | collective-permute-start | bytes 24584 | tf_op jit(solution)/shard_map/ppermute | solution.py:29
  192.0 9.2 %collective-permute-start.12 = (f32[1,1,512]{2,1,0:T(1,128)S(1)}, f32[1,1,512]{2,1,0:T(1,128)S(1)}, u32[]{:S(2)}, u32[]{:S(2)}) collective-permute-start(f32[1,1,512]{2,1,0:T(1,128)S(1)} %get-tuple-element.108), channel_id=1, source_target_pairs={{0,1},{1,2},{2,3},{3,4},{4,5},{5,6},{6,7},{7,8},{8,9},{9,10},{10,1... | collective-permute-start | bytes 6152 | tf_op jit(solution)/shard_map/ppermute | solution.py:27
  193.9 9.1 %collective-permute-start.13 = (f32[1,1,512]{2,1,0:T(1,128)S(1)}, f32[1,1,512]{2,1,0:T(1,128)S(1)}, u32[]{:S(2)}, u32[]{:S(2)}) collective-permute-start(f32[1,1,512]{2,1,0:T(1,128)S(1)} %get-tuple-element.109), channel_id=1, source_target_pairs={{1,0},{2,1},{3,2},{4,3},{5,4},{6,5},{7,6},{8,7},{9,8},{10,9},{11,1... | collective-permute-start | bytes 6152 | tf_op jit(solution)/shard_map/ppermute | solution.py:29
  203.4 9.2 %collective-permute-start.14 = (f32[4,1,512]{2,1,0:T(1,128)S(1)}, f32[4,1,512]{2,1,0:T(1,128)S(1)}, u32[]{:S(2)}, u32[]{:S(2)}) collective-permute-start(f32[4,1,512]{2,1,0:T(1,128)S(1)} %get-tuple-element.98), channel_id=1, source_target_pairs={{0,1},{1,2},{2,3},{3,4},{4,5},{5,6},{6,7},{7,8},{8,9},{9,10},{10,1... | collective-permute-start | bytes 24584 | tf_op jit(solution)/shard_map/ppermute | solution.py:27
  209.8 9.2 %collective-permute-start.15 = (f32[4,1,512]{2,1,0:T(1,128)S(1)}, f32[4,1,512]{2,1,0:T(1,128)S(1)}, u32[]{:S(2)}, u32[]{:S(2)}) collective-permute-start(f32[4,1,512]{2,1,0:T(1,128)S(1)} %get-tuple-element.99), channel_id=1, source_target_pairs={{1,0},{2,1},{3,2},{4,3},{5,4},{6,5},{7,6},{8,7},{9,8},{10,9},{11,1... | collective-permute-start | bytes 24584 | tf_op jit(solution)/shard_map/ppermute | solution.py:29
  219.3 9.2 %collective-permute-start.16 = (f32[1,1,512]{2,1,0:T(1,128)S(1)}, f32[1,1,512]{2,1,0:T(1,128)S(1)}, u32[]{:S(2)}, u32[]{:S(2)}) collective-permute-start(f32[1,1,512]{2,1,0:T(1,128)S(1)} %get-tuple-element.106), channel_id=1, source_target_pairs={{0,1},{1,2},{2,3},{3,4},{4,5},{5,6},{6,7},{7,8},{8,9},{9,10},{10,1... | collective-permute-start | bytes 6152 | tf_op jit(solution)/shard_map/ppermute | solution.py:27
  221.7 12.7 %collective-permute-start.17 = (f32[1,1,512]{2,1,0:T(1,128)S(1)}, f32[1,1,512]{2,1,0:T(1,128)S(1)}, u32[]{:S(2)}, u32[]{:S(2)}) collective-permute-start(f32[1,1,512]{2,1,0:T(1,128)S(1)} %get-tuple-element.107), channel_id=1, source_target_pairs={{1,0},{2,1},{3,2},{4,3},{5,4},{6,5},{7,6},{8,7},{9,8},{10,9},{11,1... | collective-permute-start | bytes 6152 | tf_op jit(solution)/shard_map/ppermute | solution.py:29
  234.8 9.4 %collective-permute-start.18 = (f32[4,1,512]{2,1,0:T(1,128)S(1)}, f32[4,1,512]{2,1,0:T(1,128)S(1)}, u32[]{:S(2)}, u32[]{:S(2)}) collective-permute-start(f32[4,1,512]{2,1,0:T(1,128)S(1)} %get-tuple-element.96), channel_id=1, source_target_pairs={{0,1},{1,2},{2,3},{3,4},{4,5},{5,6},{6,7},{7,8},{8,9},{9,10},{10,1... | collective-permute-start | bytes 24584 | tf_op jit(solution)/shard_map/ppermute | solution.py:27
  242.3 9.2 %collective-permute-start.19 = (f32[4,1,512]{2,1,0:T(1,128)S(1)}, f32[4,1,512]{2,1,0:T(1,128)S(1)}, u32[]{:S(2)}, u32[]{:S(2)}) collective-permute-start(f32[4,1,512]{2,1,0:T(1,128)S(1)} %get-tuple-element.97), channel_id=1, source_target_pairs={{1,0},{2,1},{3,2},{4,3},{5,4},{6,5},{7,6},{8,7},{9,8},{10,9},{11,1... | collective-permute-start | bytes 24584 | tf_op jit(solution)/shard_map/ppermute | solution.py:29
  251.7 9.2 %collective-permute-start.20 = (f32[1,1,512]{2,1,0:T(1,128)S(1)}, f32[1,1,512]{2,1,0:T(1,128)S(1)}, u32[]{:S(2)}, u32[]{:S(2)}) collective-permute-start(f32[1,1,512]{2,1,0:T(1,128)S(1)} %get-tuple-element.104), channel_id=1, source_target_pairs={{0,1},{1,2},{2,3},{3,4},{4,5},{5,6},{6,7},{7,8},{8,9},{9,10},{10,1... | collective-permute-start | bytes 6152 | tf_op jit(solution)/shard_map/ppermute | solution.py:27
  258.8 9.1 %collective-permute-start.21 = (f32[1,1,512]{2,1,0:T(1,128)S(1)}, f32[1,1,512]{2,1,0:T(1,128)S(1)}, u32[]{:S(2)}, u32[]{:S(2)}) collective-permute-start(f32[1,1,512]{2,1,0:T(1,128)S(1)} %get-tuple-element.105), channel_id=1, source_target_pairs={{1,0},{2,1},{3,2},{4,3},{5,4},{6,5},{7,6},{8,7},{9,8},{10,9},{11,1... | collective-permute-start | bytes 6152 | tf_op jit(solution)/shard_map/ppermute | solution.py:29
  292.7 4.3 %collective-permute-start.22 = (f32[2,1,64]{2,1,0:T(1,128)S(1)}, f32[2,1,64]{2,1,0:T(1,128)S(1)}, u32[]{:S(2)}, u32[]{:S(2)}) collective-permute-start(f32[2,1,64]{2,1,0:T(1,128)S(1)} %get-tuple-element.94), channel_id=1, source_target_pairs={{0,8},{8,16},{16,24},{24,32},{32,40},{40,48},{48,56},{56,64},{64,7... | collective-permute-start | bytes 1544 | tf_op jit(solution)/shard_map/ppermute | solution.py:27
  294.6 6.1 %collective-permute-start.23 = (f32[2,1,64]{2,1,0:T(1,128)S(1)}, f32[2,1,64]{2,1,0:T(1,128)S(1)}, u32[]{:S(2)}, u32[]{:S(2)}) collective-permute-start(f32[2,1,64]{2,1,0:T(1,128)S(1)} %get-tuple-element.95), channel_id=1, source_target_pairs={{8,0},{16,8},{24,16},{32,24},{40,32},{48,40},{56,48},{64,56},{72,6... | collective-permute-start | bytes 1544 | tf_op jit(solution)/shard_map/ppermute | solution.py:29
  300.8 9.2 %collective-permute-start.24 = (f32[2,34,1]{2,1,0:T(8,128)S(1)}, f32[2,34,1]{2,1,0:T(8,128)S(1)}, u32[]{:S(2)}, u32[]{:S(2)}) collective-permute-start(f32[2,34,1]{2,1,0:T(8,128)S(1)} %get-tuple-element.92), channel_id=1, source_target_pairs={{0,1},{1,2},{2,3},{3,4},{4,5},{5,6},{6,7},{8,9},{9,10},{10,11},{11... | collective-permute-start | bytes 824 | tf_op jit(solution)/shard_map/ppermute | solution.py:27
  307.8 9.6 %collective-permute-start.25 = (f32[2,34,1]{2,1,0:T(8,128)S(1)}, f32[2,34,1]{2,1,0:T(8,128)S(1)}, u32[]{:S(2)}, u32[]{:S(2)}) collective-permute-start(f32[2,34,1]{2,1,0:T(8,128)S(1)} %get-tuple-element.93), channel_id=1, source_target_pairs={{1,0},{2,1},{3,2},{4,3},{5,4},{6,5},{7,6},{9,8},{10,9},{11,10},{12... | collective-permute-start | bytes 824 | tf_op jit(solution)/shard_map/ppermute | solution.py:29
where the time goes:
time: 320 us; the launch traced here: 319 us
  starting transfers between devices  113 us (35%)
  waiting for transfers between devices  80.1 us (25%)
  local copies, waits for them, and re-layouts  79 us (25%)
  blocking collectives  34.3 us (11%)
  other arithmetic  9.37 us (3%)
    ppermute x13, waiting for transfers between devices, padded_2(): lax.ppermute(head, axis, [((i + 1) % count, i) for i in range(ends)])  68.7 us
    ppermute x13, starting transfers between devices, padded_2(): lax.ppermute(tail, axis, [(i, (i + 1) % count) for i in range(ends)])  67 us
    another operation x12, local copies, waits for them, and re-layouts, radiation(): jnp.stack([water_depth * along_speed * along_speed + potential_part, wate...  52.5 us
    ppermute x13, starting transfers between devices, padded_2(): lax.ppermute(head, axis, [((i + 1) % count, i) for i in range(ends)])  46.5 us
    all_to_all x1, blocking collectives, per_device(): lax.all_to_all(slab_flows, 'cross', split_axis=2, concat_axis=1, tiled=True)  21.7 us
    concatenate x4, local copies, waits for them, and re-layouts, per_device(): jnp.concatenate([stress, jnp.stack([water_depth, wet_share])], axis=0)  17.4 us
    all_to_all x1, blocking collectives, per_device(): lax.all_to_all(restrict(fields), 'cross', split_axis=1, concat_axis=2, ti...  12.7 us
    ppermute x13, waiting for transfers between devices, padded_2(): lax.ppermute(tail, axis, [(i, (i + 1) % count) for i in range(ends)])  11.3 us
  transfers between devices with their start and end apart: 26, of which 12 were waited for; matrix products, arithmetic and copies ran while one was open for 11% of the time, Pallas kernels for 0%

commit v1 on v0

v1 whole, which is shorter than its diff:
```python
import functools

import jax
import jax.numpy as jnp
from jax import lax
from jax.experimental import pallas as pl
from jax.experimental.pallas import tpu as pltpu
from jax.sharding import PartitionSpec as P

STEPS = 2
CIRC = 3
CONTINUITY = 0.25
MOMENTUM = 0.3
POTENTIAL = 0.5
CIRC_LEVEL = 0.2
CIRC_FORCE = 0.3
FRICTION = 0.1
VISCOSITY = 0.1

MESH = pl.DeviceIdType.MESH
F32 = jnp.float32
BF16 = jnp.bfloat16

TR = 128
TC = 256
TOP = 16
ER = TR + 2 * TOP
EC = TC + 128
CR = TR // 4
CC = TC // 4
WR = CR + 16
CHUNK = 32
OWN = [(r, CHUNK) for r in range(TOP, TOP + TR, CHUNK)]
ALL = [(TOP - 8, 8)] + OWN + [(TOP + TR, 8)]
DIRS = [(0, -1), (0, 1), (-1, -1), (-1, 1), (1, -1), (1, 1), (-1, 0), (1, 0)]


def iota(shape, dim):
    return lax.broadcasted_iota(jnp.int32, shape, dim)


def halves(x):
    high = x.astype(BF16)
    return high, (x - high.astype(F32)).astype(BF16)


def dot(x, y):
    return jnp.dot(x, y, preferred_element_type=F32)


def dot_nt(x, y):
    return lax.dot_general(x, y, (((1,), (1,)), ((), ())), preferred_element_type=F32)


def row_next(x, keep):
    return pltpu.roll(x, x.shape[0] - 1, 0)[keep]


def row_prev(x, keep):
    return pltpu.roll(x, 1, 0)[keep]


def col_next(x):
    return pltpu.roll(x, x.shape[1] - 1, 1)


def col_prev(x):
    return pltpu.roll(x, 1, 1)


def spread(fine, coarse, fine_dim, shape, first, wrap):
    f = iota(shape, fine_dim)
    c = iota(shape, 1 - fine_dim)
    base = lax.shift_right_logical(f, 2) + first
    k = f & 3
    weight = jnp.where((k == 0) | (k == 3), 0.375, 0.125)
    other = base + jnp.where(k < 2, -1, 1)
    if wrap:
        other = other & (coarse - 1)
    zero = jnp.zeros(shape, F32)
    return (jnp.where(c == base, 1.0 - weight, zero) + jnp.where(c == other, weight, zero)).astype(BF16)


def kernel(
    mesh_rows, mesh_cols,
    s_in, u_in, v_in, d_in, w_in, cells_ref, press_ref,
    s_out, u_out, v_out, ca_out, cc_out,
    ext, speed, wraw, forc, r1, r2, curv, planes, pack, packt, got, corner,
    ts_w, ts_s, side_w, side_s, cw, cs, cur,
    load_sem, store_sem, f_send, f_recv, w_send, w_recv, c_send, c_recv,
):
    a = lax.axis_index("along")
    c = lax.axis_index("cross")
    total_cols = TC * mesh_cols

    def there(da, dc):
        ok = None
        for cond in ([a > 0] if da < 0 else [a < mesh_rows - 1] if da > 0 else []) + (
            [c > 0] if dc < 0 else [c < mesh_cols - 1] if dc > 0 else []
        ):
            ok = cond if ok is None else ok & cond
        return ok

    def device(da, dc):
        return (a + da, c + dc)

    loads = []
    for k, src in enumerate((s_in, u_in, v_in, d_in)):
        loads.append(pltpu.make_async_copy(src, ext.at[k, TOP:TOP + TR, 0:TC], load_sem.at[k]))
    loads.append(pltpu.make_async_copy(w_in, wraw, load_sem.at[4]))
    for cp in loads:
        cp.start()

    for f in range(5):
        ext[f, 0:TOP, :] = jnp.zeros((TOP, EC), F32)
        ext[f, TOP + TR:ER, :] = jnp.zeros((TOP, EC), F32)
    for ref in (r1, r2, curv, speed.at[0], speed.at[1]):
        ref[0:8, :] = jnp.zeros((8, EC), F32)
        ref[ER - 8:ER, :] = jnp.zeros((8, EC), F32)
    got[...] = jnp.zeros_like(got)
    corner[...] = jnp.zeros_like(corner)
    side_w[...] = jnp.zeros_like(side_w)
    side_s[...] = jnp.zeros_like(side_s)
    for ref, nf in ((cw, 2), (cs, 3)):
        for f in range(nf):
            ref[f, 0:8, :] = jnp.zeros((8, 128), F32)
            ref[f, WR - 8:WR, :] = jnp.zeros((8, 128), F32)

    barrier = pltpu.get_barrier_semaphore()
    for da, dc in DIRS:
        @pl.when(there(da, dc))
        def _(da=da, dc=dc):
            pl.semaphore_signal(barrier, inc=1, device_id=device(da, dc), device_id_type=MESH)
    rows_near = 1 + jnp.where(a > 0, 1, 0) + jnp.where(a < mesh_rows - 1, 1, 0)
    cols_near = 1 + jnp.where(c > 0, 1, 0) + jnp.where(c < mesh_cols - 1, 1, 0)
    pl.semaphore_wait(barrier, rows_near * cols_near - 1)

    for cp in loads:
        cp.wait()
    ext[4, TOP:TOP + TR, 0:TC] = wraw[...].astype(F32)

    lane = iota((TR, 128), 1)
    packed = jnp.zeros((TR, 128), F32)
    for f in range(5):
        left = ext[f, TOP:TOP + TR, 0:128]
        right = ext[f, TOP:TOP + TR, TC - 128:TC]
        edge = pltpu.roll(jnp.where(lane >= 120, right, left), 16 * f + 8, 1)
        packed = jnp.where(lax.shift_right_logical(lane, 4) == f, edge, packed)
    pack[...] = packed
    packt[...] = packed.T.reshape(8, 2, 8, 128)

    def fine_copy(n):
        da, dc = DIRS[n]
        if da == 0:
            which = 0 if dc > 0 else 1
            src, dst = packt.at[0:5, which], got.at[0:5, which]
        elif dc == 0:
            src = ext.at[:, TOP:TOP + 8, 0:TC] if da < 0 else ext.at[:, TOP + TR - 8:TOP + TR, 0:TC]
            dst = ext.at[:, TOP + TR:TOP + TR + 8, 0:TC] if da < 0 else ext.at[:, TOP - 8:TOP, 0:TC]
        else:
            src = pack.at[0:8] if da < 0 else pack.at[TR - 8:TR]
            dst = corner.at[1 if da < 0 else 0, 0 if dc > 0 else 1]
        return pltpu.make_async_remote_copy(
            src_ref=src, dst_ref=dst, send_sem=f_send.at[n], recv_sem=f_recv.at[n],
            device_id=device(da, dc), device_id_type=MESH)

    def coarse_copy(ts, side, field, send, recv):
        def make(n):
            da, dc = DIRS[n]
            if dc == 0:
                src = field.at[:, 8:16] if da < 0 else field.at[:, CR:CR + 8]
                dst = field.at[:, CR + 8:CR + 16] if da < 0 else field.at[:, 0:8]
            else:
                src = ts.at[0 if dc < 0 else 1]
                at = CC if dc < 0 else 120
                dst = side.at[{-1: 2, 0: 1, 1: 0}[da], at:at + 8]
            return pltpu.make_async_remote_copy(
                src_ref=src, dst_ref=dst, send_sem=send.at[n], recv_sem=recv.at[n],
                device_id=device(da, dc), device_id_type=MESH)
        return make

    def start_all(make):
        for n, (da, dc) in enumerate(DIRS):
            @pl.when(there(da, dc))
            def _(n=n):
                make(n).start()

    def wait_recv_all(make):
        for n, (da, dc) in enumerate(DIRS):
            @pl.when(there(-da, -dc))
            def _(n=n):
                make(n).wait_recv()

    def wait_send_all(make):
        for n, (da, dc) in enumerate(DIRS):
            @pl.when(there(da, dc))
            def _(n=n):
                make(n).wait_send()

    copy_w = coarse_copy(ts_w, side_w, cw, w_send, w_recv)
    copy_s = coarse_copy(ts_s, side_s, cs, c_send, c_recv)
    start_all(fine_copy)

    pool = (lax.shift_right_logical(iota((TC, 128), 0), 2) == iota((TC, 128), 1)).astype(F32).astype(BF16)
    edge_row = iota((16, TC), 0)
    edge_row = jnp.where(edge_row < 8, edge_row, edge_row + (CC - 16))
    pool_edge = (lax.shift_right_logical(iota((16, TC), 1), 2) == edge_row).astype(F32).astype(BF16)

    def restrict(first, nf, scale, ts, field):
        tall = []
        for f in range(nf):
            wide = []
            for h in range(2):
                n = 2 * (first + f) + h
                total = planes[n, pl.ds(0, CR, stride=4), :]
                for k in range(1, 4):
                    total = total + planes[n, pl.ds(k, CR, stride=4), :]
                wide.append(total * scale)
            tall.append(jnp.concatenate(wide, axis=1))
        tall.append(jnp.zeros((TR - nf * CR, TC), F32))
        high, low = halves(jnp.concatenate(tall, axis=0))
        edges = dot_nt(pool_edge, high) + dot_nt(pool_edge, low)
        ts[0] = edges[0:8]
        ts[1] = edges[8:16]
        coarse = dot(high, pool) + dot(low, pool)
        for f in range(nf):
            field[f, 8:8 + CR] = coarse[f * CR:(f + 1) * CR]

    def widen(field, side, nf):
        up, mid, down = (side[k].T for k in range(3))
        out = []
        for f in range(nf):
            r = f * CR
            out.append(jnp.concatenate([
                field[f, 0:8] + up[r + CR - 8:r + CR],
                field[f, 8:8 + CR] + mid[r:r + CR],
                field[f, CR + 8:WR] + down[r:r + 8],
            ], axis=0))
        return out

    for h in range(2):
        planes[6 + h] = ext[3, TOP:TOP + TR, 128 * h:128 * h + 128]
        planes[8 + h] = ext[4, TOP:TOP + TR, 128 * h:128 * h + 128]
    restrict(3, 2, 1.0 / 16.0, ts_w, cw)
    start_all(copy_w)

    ext_row = a * TR - TOP + iota((ER, 8), 0)
    ext_col = iota((EC, 8), 0)
    ext_col = c * TC + jnp.where(ext_col < TC + 64, ext_col, ext_col - EC)
    for step in range(STEPS):
        cells = cells_ref[step:step + 1, :]
        row_hit = jnp.where(ext_row == lax.div(cells, total_cols), press_ref[...], 0.0)
        col_hit = jnp.where(ext_col == lax.rem(cells, total_cols), 1.0, 0.0)
        forc[step] = lax.dot_general(
            row_hit, col_hit, (((1,), (1,)), ((), ())),
            precision=lax.Precision.HIGHEST, preferred_element_type=F32)

    wait_recv_all(fine_copy)
    is_right = (lane & 15) >= 8
    mid = got[...].reshape(TR, 128).T
    top = jnp.where(is_right[0:8], corner[0, 1], corner[0, 0])
    bottom = jnp.where(is_right[0:8], corner[1, 1], corner[1, 0])
    halo = jnp.concatenate([top, mid, bottom], axis=0)
    halo_lane = iota((TR + 16, 128), 1)
    for f in range(5):
        moved = pltpu.roll(halo, 120 - 16 * f, 1)
        ext[f, TOP - 8:TOP + TR + 8, TC:EC] = jnp.where((halo_lane < 8) | (halo_lane >= 120), moved, 0.0)

    surface, along, cross = ext.at[0], ext.at[1], ext.at[2]
    for step in range(STEPS):
        raised = r1 if step == 0 else r2
        for r, n in ALL:
            keep = slice(8, 8 + n)
            wide = slice(r - 8, r + n + 8)
            here = slice(r, r + n)
            depth = ext[3, wide, :]
            du = depth * along[wide, :]
            dv = depth[keep] * cross[here, :]
            flux = (row_next(du, keep) - row_prev(du, keep)) + (col_next(dv) - col_prev(dv))
            raised[here, :] = ext[4, here, :] * (
                surface[here, :] - (0.5 * CONTINUITY) * flux + forc[step, here, :])
        if step == STEPS - 1:
            surface_store = pltpu.make_async_copy(
                raised.at[TOP:TOP + TR, 0:TC], s_out, store_sem.at[0])
            surface_store.start()
        for r, n in ALL:
            keep = slice(8, 8 + n)
            x = raised[r - 8:r + n + 8, :]
            mid = x[keep]
            curv[r:r + n, :] = (
                row_next(x, keep) + row_prev(x, keep) + col_next(mid) + col_prev(mid) - 4.0 * mid)
        for r, n in (ALL if step < STEPS - 1 else OWN):
            keep = slice(8, 8 + n)
            here = slice(r, r + n)
            x = raised[r - 8:r + n + 8, :]
            k = curv[r - 8:r + n + 8, :]
            depth = ext[3, here, :]
            wet = ext[4, here, :]
            disp = depth * depth * (1.0 / 3.0)
            push_a = (row_next(x, keep) - row_prev(x, keep)) + disp * (row_next(k, keep) - row_prev(k, keep))
            x = x[keep]
            k = k[keep]
            push_c = (col_next(x) - col_prev(x)) + disp * (col_next(k) - col_prev(k))
            u = wet * (along[here, :] - (0.5 * MOMENTUM) * push_a)
            v = wet * (cross[here, :] - (0.5 * MOMENTUM) * push_c)
            speed[0, here, :] = u
            speed[1, here, :] = v
            if (r, n) in OWN:
                pot = POTENTIAL * x * x
                stress = (depth * u * u + pot, depth * u * v, depth * v * v + pot)
                at = slice(r - TOP, r - TOP + n)
                for f in range(3):
                    for h in range(2):
                        part = stress[f][:, 128 * h:128 * h + 128]
                        if step > 0:
                            part = part + planes[2 * f + h, at]
                        planes[2 * f + h, at] = part
        surface, along, cross = raised, speed.at[0], speed.at[1]

    restrict(0, 3, 1.0 / (16.0 * STEPS), ts_s, cs)
    start_all(copy_s)
    speed_stores = [
        pltpu.make_async_copy(speed.at[0, TOP:TOP + TR, 0:TC], u_out, store_sem.at[1]),
        pltpu.make_async_copy(speed.at[1, TOP:TOP + TR, 0:TC], v_out, store_sem.at[2]),
    ]
    for cp in speed_stores:
        cp.start()

    cols_out = spread(TC, 128, 1, (128, TC), 0, True)
    cols_out = jnp.concatenate([cols_out, cols_out], axis=0)
    rows_out = spread(TR, WR, 0, (TR, WR), 8, False)
    rows_out = jnp.concatenate([rows_out, rows_out], axis=1)
    wait_recv_all(copy_w)
    depth, wet = widen(cw, side_w, 2)
    inside = depth > 0.25
    inv_depth = 1.0 / jnp.maximum(depth, 0.25)

    wait_recv_all(copy_s)
    s0, s1, s2 = widen(cs, side_s, 3)

    def dr(x):
        return 0.5 * (pltpu.roll(x, WR - 1, 0) - pltpu.roll(x, 1, 0))

    def dc(x):
        return 0.5 * (col_next(x) - col_prev(x))

    def laplace(x):
        return pltpu.roll(x, WR - 1, 0) + pltpu.roll(x, 1, 0) + col_next(x) + col_prev(x) - 4.0 * x

    force_a = -(dr(s0) + dc(s1)) * inv_depth
    force_c = -(dr(s1) + dc(s2)) * inv_depth
    flow_a = wet * (CIRC_FORCE * force_a)
    flow_c = wet * (CIRC_FORCE * force_c)
    elevation = jnp.zeros_like(depth)
    for _ in range(CIRC - 1):
        level = elevation - CIRC_LEVEL * (dr(depth * flow_a) + dc(depth * flow_c))
        elevation = jnp.where(inside, level, 0.0)
        flow_a, flow_c = (
            wet * (flow_a + CIRC_FORCE * (force_a - dr(elevation))
                   - FRICTION * flow_a * inv_depth + VISCOSITY * laplace(flow_a)),
            wet * (flow_c + CIRC_FORCE * (force_c - dc(elevation))
                   - FRICTION * flow_c * inv_depth + VISCOSITY * laplace(flow_c)),
        )

    high, low = halves(jnp.concatenate([flow_a, flow_c], axis=0))
    wide = dot(jnp.concatenate([high, low], axis=1), cols_out)
    high, low = halves(jnp.concatenate([wide[0:WR], wide[WR:2 * WR]], axis=1))
    fine = dot(rows_out, jnp.concatenate([high, low], axis=0))
    mask = ext[4, TOP:TOP + TR, 0:TC]
    cur[0] = fine[:, 0:TC] * mask
    cur[1] = fine[:, TC:2 * TC] * mask
    last = [
        pltpu.make_async_copy(cur.at[0], ca_out, store_sem.at[3]),
        pltpu.make_async_copy(cur.at[1], cc_out, store_sem.at[4]),
    ]
    for cp in last:
        cp.start()
    surface_store.wait()
    for cp in speed_stores:
        cp.wait()
    wait_send_all(fine_copy)
    wait_send_all(copy_w)
    wait_send_all(copy_s)
    for cp in last:
        cp.wait()


def solution(mesh):
    mesh_rows, mesh_cols = mesh.shape["along"], mesh.shape["cross"]
    hbm = pl.BlockSpec(memory_space=pl.ANY)
    vmem = pl.BlockSpec(memory_space=pltpu.VMEM)

    def per_device(surface, along_speed, cross_speed, water_depth, wet_mask, ship_cells, ship_pressure):
        tile = jax.ShapeDtypeStruct((TR, TC), F32)
        sems = [pltpu.SemaphoreType.DMA((8,))] * 6
        return pl.pallas_call(
            functools.partial(kernel, mesh_rows, mesh_cols),
            out_shape=[tile] * 5,
            in_specs=[hbm] * 5 + [vmem] * 2,
            out_specs=[hbm] * 5,
            scratch_shapes=[
                pltpu.VMEM((5, ER, EC), F32),
                pltpu.VMEM((2, ER, EC), F32),
                pltpu.VMEM((TR, TC), jnp.int32),
                pltpu.VMEM((STEPS, ER, EC), F32),
                pltpu.VMEM((ER, EC), F32),
                pltpu.VMEM((ER, EC), F32),
                pltpu.VMEM((ER, EC), F32),
                pltpu.VMEM((10, TR, 128), F32),
                pltpu.VMEM((TR, 128), F32),
                pltpu.VMEM((8, 2, 8, 128), F32),
                pltpu.VMEM((8, 2, 8, 128), F32),
                pltpu.VMEM((2, 2, 8, 128), F32),
                pltpu.VMEM((2, 8, 128), F32),
                pltpu.VMEM((2, 8, 128), F32),
                pltpu.VMEM((3, 128, 128), F32),
                pltpu.VMEM((3, 128, 128), F32),
                pltpu.VMEM((2, WR, 128), F32),
                pltpu.VMEM((3, WR, 128), F32),
                pltpu.VMEM((2, TR, TC), F32),
                pltpu.SemaphoreType.DMA((5,)),
                pltpu.SemaphoreType.DMA((5,)),
            ] + sems,
            compiler_params=pltpu.CompilerParams(
                collective_id=0, has_side_effects=True, vmem_limit_bytes=32 * 1024 * 1024),
        )(surface, along_speed, cross_speed, water_depth, wet_mask, ship_cells,
          ship_pressure.reshape(1, ship_pressure.shape[0]))

    tiled = P("along", "cross")
    return jax.shard_map(
        per_device,
        mesh=mesh,
        in_specs=(tiled,) * 5 + (P(), P()),
        out_specs=(tiled,) * 5,
        check_vma=False,
    )
```

time: 320 us -> 38.7 us (0.12)
  the two profiles are of different devices: /device:TPU:233 before, /device:TPU:22 now
where the time goes in v1:
time: 38.7 us; the launch traced here: 38.4 us
  Pallas kernels  29.3 us (76%)
  local copies, waits for them, and re-layouts  8.47 us (22%)
  between operations  0.67 us (2%)
    pallas_call x1, Pallas kernels, per_device(): pl.pallas_call(functools.partial(kernel, mesh_rows, mesh_cols), out_shape...  29.3 us
    unnamed x19, local copies, waits for them, and re-layouts  8.47 us

profile of v1, /device:TPU:22, one launch (start us, length us, event | category | flops | bytes accessed | tf_op | source)
XLA Modules:
  0.0 38.4 jit_solution(3458044761016783147)
XLA Ops:
  0.6 0.0 copy-start.6
  0.6 0.0 copy-start.5
  0.7 0.6 %copy-done.6 = f32[8]{0:T(128)S(1)} copy-done((f32[8]{0:T(128)S(1)}, f32[8]{0:T(128)}, u32[]{:S(2)}) %copy-start.6) | copy-done | bytes 56
  1.3 0.0 copy-done.5
  1.3 0.0 copy-start
  1.3 0.9 %copy-done = f32[128,256]{1,0:T(8,128)S(1)} copy-done((f32[128,256]{1,0:T(8,128)S(1)}, f32[128,256]{1,0:T(8,128)}, u32[]{:S(2)}) %copy-start) | copy-done | bytes 131096
  2.2 0.0 copy-start.1
  2.2 0.9 %copy-done.1 = f32[128,256]{1,0:T(8,128)S(1)} copy-done((f32[128,256]{1,0:T(8,128)S(1)}, f32[128,256]{1,0:T(8,128)}, u32[]{:S(2)}) %copy-start.1) | copy-done | bytes 131096
  3.1 0.0 copy-start.2
  3.1 0.9 %copy-done.2 = f32[128,256]{1,0:T(8,128)S(1)} copy-done((f32[128,256]{1,0:T(8,128)S(1)}, f32[128,256]{1,0:T(8,128)}, u32[]{:S(2)}) %copy-start.2) | copy-done | bytes 131096
  4.0 0.0 copy-start.3
  4.0 0.9 %copy-done.3 = f32[128,256]{1,0:T(8,128)S(1)} copy-done((f32[128,256]{1,0:T(8,128)S(1)}, f32[128,256]{1,0:T(8,128)}, u32[]{:S(2)}) %copy-start.3) | copy-done | bytes 131096
  4.9 0.0 copy-start.4
  5.0 0.9 %copy-done.4 = s32[128,256]{1,0:T(8,128)S(1)} copy-done((s32[128,256]{1,0:T(8,128)S(1)}, s32[128,256]{1,0:T(8,128)}, u32[]{:S(2)}) %copy-start.4) | copy-done | bytes 131096
  5.9 29.3 %shard_map.110 = (f32[128,256]{1,0:T(8,128)S(1)}, f32[128,256]{1,0:T(8,128)S(1)}, f32[128,256]{1,0:T(8,128)S(1)}, f32[128,256]{1,0:T(8,128)S(1)}, f32[128,256]{1,0:T(8,128)S(1)}) custom-call(f32[128,256]{1,0:T(8,128)S(1)} %copy-done, f32[128,256]{1,0:T(8,128)S(1)} %copy-done.1, f32[128,256]{1,0:T(8,128)S(1)} %copy-done.2, f32[128,256]{1,0:T(8,128)S(1)} %copy-done.3, ...), custom_call_target="tpu_custom_call" | custom-call | tf_op jit(solution)/shard_map/pallas_call | solution.py:396
  35.1 0.7 %copy.17 = f32[128,256]{1,0:T(8,128)} copy(f32[128,256]{1,0:T(8,128)S(1)} %get-tuple-element.10) | data formatting | bytes 262144
  35.8 0.7 %copy.18 = f32[128,256]{1,0:T(8,128)} copy(f32[128,256]{1,0:T(8,128)S(1)} %get-tuple-element.11) | data formatting | bytes 262144
  36.5 0.7 %copy.19 = f32[128,256]{1,0:T(8,128)} copy(f32[128,256]{1,0:T(8,128)S(1)} %get-tuple-element.12) | data formatting | bytes 262144
  37.1 0.7 %copy.20 = f32[128,256]{1,0:T(8,128)} copy(f32[128,256]{1,0:T(8,128)S(1)} %get-tuple-element.13) | data formatting | bytes 262144
  37.8 0.7 %copy.21 = f32[128,256]{1,0:T(8,128)} copy(f32[128,256]{1,0:T(8,128)S(1)} %get-tuple-element.14) | data formatting | bytes 262144
Async XLA Ops:
  0.6 0.7 %copy-start.6 = (f32[8]{0:T(128)S(1)}, f32[8]{0:T(128)}, u32[]{:S(2)}) copy-start(f32[8]{0:T(128)} %param.13) | copy-start | bytes 100
  0.6 0.7 %copy-start.5 = (s32[2,8]{1,0:T(2,128)S(1)}, s32[2,8]{1,0:T(2,128)}, u32[]{:S(2)}) copy-start(s32[2,8]{1,0:T(2,128)} %cells_ref.1) | copy-start | bytes 196
  1.3 0.9 %copy-start = (f32[128,256]{1,0:T(8,128)S(1)}, f32[128,256]{1,0:T(8,128)}, u32[]{:S(2)}) copy-start(f32[128,256]{1,0:T(8,128)} %s_in.1) | copy-start | bytes 393220
  2.2 0.9 %copy-start.1 = (f32[128,256]{1,0:T(8,128)S(1)}, f32[128,256]{1,0:T(8,128)}, u32[]{:S(2)}) copy-start(f32[128,256]{1,0:T(8,128)} %u_in.1) | copy-start | bytes 393220
  3.1 0.9 %copy-start.2 = (f32[128,256]{1,0:T(8,128)S(1)}, f32[128,256]{1,0:T(8,128)}, u32[]{:S(2)}) copy-start(f32[128,256]{1,0:T(8,128)} %v_in.1) | copy-start | bytes 393220
  4.0 0.9 %copy-start.3 = (f32[128,256]{1,0:T(8,128)S(1)}, f32[128,256]{1,0:T(8,128)}, u32[]{:S(2)}) copy-start(f32[128,256]{1,0:T(8,128)} %d_in.1) | copy-start | bytes 393220
  4.9 0.9 %copy-start.4 = (s32[128,256]{1,0:T(8,128)S(1)}, s32[128,256]{1,0:T(8,128)}, u32[]{:S(2)}) copy-start(s32[128,256]{1,0:T(8,128)} %w_in.1) | copy-start | bytes 393220

commit v2 on v1

--- a/solution.py
+++ b/solution.py
@@ -83,15 +83,16 @@
 
 def kernel(
     mesh_rows, mesh_cols,
-    s_in, u_in, v_in, d_in, w_in, cells_ref, press_ref,
-    s_out, u_out, v_out, ca_out, cc_out,
-    ext, speed, wraw, forc, r1, r2, curv, planes, pack, packt, got, corner,
-    ts_w, ts_s, side_w, side_s, cw, cs, cur,
-    load_sem, store_sem, f_send, f_recv, w_send, w_recv, c_send, c_recv,
+    s_in, u_in, v_in, d_in, w_in, cells_in, press_in,
+    r2, u_out, v_out, flow_out, mask_out,
+    ext, wraw, cells_ref, press_ref, forc, r1, curv, planes, pack, packt, got, corner,
+    ts_w, ts_s, side_w, side_s, cw, cs,
+    load_sem, f_send, f_recv, w_send, w_recv, c_send, c_recv,
 ):
     a = lax.axis_index("along")
     c = lax.axis_index("cross")
     total_cols = TC * mesh_cols
+    outs = (r2, u_out, v_out)
 
     def there(da, dc):
         ok = None
@@ -104,40 +105,60 @@
     def device(da, dc):
         return (a + da, c + dc)
 
-    loads = []
-    for k, src in enumerate((s_in, u_in, v_in, d_in)):
-        loads.append(pltpu.make_async_copy(src, ext.at[k, TOP:TOP + TR, 0:TC], load_sem.at[k]))
-    loads.append(pltpu.make_async_copy(w_in, wraw, load_sem.at[4]))
-    for cp in loads:
-        cp.start()
-
-    for f in range(5):
-        ext[f, 0:TOP, :] = jnp.zeros((TOP, EC), F32)
-        ext[f, TOP + TR:ER, :] = jnp.zeros((TOP, EC), F32)
-    for ref in (r1, r2, curv, speed.at[0], speed.at[1]):
-        ref[0:8, :] = jnp.zeros((8, EC), F32)
-        ref[ER - 8:ER, :] = jnp.zeros((8, EC), F32)
-    got[...] = jnp.zeros_like(got)
-    corner[...] = jnp.zeros_like(corner)
-    side_w[...] = jnp.zeros_like(side_w)
-    side_s[...] = jnp.zeros_like(side_s)
-    for ref, nf in ((cw, 2), (cs, 3)):
-        for f in range(nf):
-            ref[f, 0:8, :] = jnp.zeros((8, 128), F32)
-            ref[f, WR - 8:WR, :] = jnp.zeros((8, 128), F32)
-
     barrier = pltpu.get_barrier_semaphore()
     for da, dc in DIRS:
         @pl.when(there(da, dc))
         def _(da=da, dc=dc):
             pl.semaphore_signal(barrier, inc=1, device_id=device(da, dc), device_id_type=MESH)
+
+    loads = []
+    for k, src in enumerate((s_in, u_in, v_in, d_in)):
+        loads.append(pltpu.make_async_copy(src, ext.at[k, TOP:TOP + TR, 0:TC], load_sem.at[k]))
+    loads.append(pltpu.make_async_copy(w_in, wraw, load_sem.at[4]))
+    loads.append(pltpu.make_async_copy(cells_in, cells_ref, load_sem.at[5]))
+    loads.append(pltpu.make_async_copy(press_in, press_ref, load_sem.at[6]))
+    for cp in loads:
+        cp.start()
+
+    for f in range(5):
+        ext[f, 0:8, :] = jnp.zeros((8, EC), F32)
+        ext[f, ER - 8:ER, :] = jnp.zeros((8, EC), F32)
+    for ref in (r1, curv, *outs):
+        ref[0:8, :] = jnp.zeros((8, EC), F32)
+        ref[ER - 8:ER, :] = jnp.zeros((8, EC), F32)
+    for side in (side_w, side_s):
+        for k in range(3):
+            side[k, 0:CC] = jnp.zeros((CC, 128), F32)
+            side[k, CC + 8:120] = jnp.zeros((112 - CC, 128), F32)
+    for da, dc in DIRS:
+        @pl.when(jnp.logical_not(there(da, dc)))
+        def _(da=da, dc=dc):
+            if dc == 0:
+                at = TOP - 8 if da < 0 else TOP + TR
+                for f in range(5):
+                    ext[f, at:at + 8, 0:TC] = jnp.zeros((8, TC), F32)
+                at = 0 if da < 0 else WR - 8
+                for ref, nf in ((cw, 2), (cs, 3)):
+                    for f in range(nf):
+                        ref[f, at:at + 8] = jnp.zeros((8, 128), F32)
+                return
+            right = 1 if dc > 0 else 0
+            if da == 0:
+                for f in range(5):
+                    got[f, right] = jnp.zeros((8, 128), F32)
+            else:
+                corner[0 if da < 0 else 1, right] = jnp.zeros((8, 128), F32)
+            at = CC if right else 120
+            for side in (side_w, side_s):
+                side[da + 1, at:at + 8] = jnp.zeros((8, 128), F32)
+
     rows_near = 1 + jnp.where(a > 0, 1, 0) + jnp.where(a < mesh_rows - 1, 1, 0)
     cols_near = 1 + jnp.where(c > 0, 1, 0) + jnp.where(c < mesh_cols - 1, 1, 0)
-    pl.semaphore_wait(barrier, rows_near * cols_near - 1)
-
     for cp in loads:
         cp.wait()
-    ext[4, TOP:TOP + TR, 0:TC] = wraw[...].astype(F32)
+    own_wet = wraw[...].astype(F32)
+    ext[4, TOP:TOP + TR, 0:TC] = own_wet
+    mask_out[...] = own_wet
 
     lane = iota((TR, 128), 1)
     packed = jnp.zeros((TR, 128), F32)
@@ -197,6 +218,7 @@
             def _(n=n):
                 make(n).wait_send()
 
+    pl.semaphore_wait(barrier, rows_near * cols_near - 1)
     copy_w = coarse_copy(ts_w, side_w, cw, w_send, w_recv)
     copy_s = coarse_copy(ts_s, side_s, cs, c_send, c_recv)
     start_all(fine_copy)
@@ -279,10 +301,6 @@
             flux = (row_next(du, keep) - row_prev(du, keep)) + (col_next(dv) - col_prev(dv))
             raised[here, :] = ext[4, here, :] * (
                 surface[here, :] - (0.5 * CONTINUITY) * flux + forc[step, here, :])
-        if step == STEPS - 1:
-            surface_store = pltpu.make_async_copy(
-                raised.at[TOP:TOP + TR, 0:TC], s_out, store_sem.at[0])
-            surface_store.start()
         for r, n in ALL:
             keep = slice(8, 8 + n)
             x = raised[r - 8:r + n + 8, :]
@@ -303,8 +321,8 @@
             push_c = (col_next(x) - col_prev(x)) + disp * (col_next(k) - col_prev(k))
             u = wet * (along[here, :] - (0.5 * MOMENTUM) * push_a)
             v = wet * (cross[here, :] - (0.5 * MOMENTUM) * push_c)
-            speed[0, here, :] = u
-            speed[1, here, :] = v
+            u_out[here, :] = u
+            v_out[here, :] = v
             if (r, n) in OWN:
                 pot = POTENTIAL * x * x
                 stress = (depth * u * u + pot, depth * u * v, depth * v * v + pot)
@@ -315,21 +333,10 @@
                         if step > 0:
                             part = part + planes[2 * f + h, at]
                         planes[2 * f + h, at] = part
-        surface, along, cross = raised, speed.at[0], speed.at[1]
+        surface, along, cross = raised, u_out, v_out
 
     restrict(0, 3, 1.0 / (16.0 * STEPS), ts_s, cs)
     start_all(copy_s)
-    speed_stores = [
-        pltpu.make_async_copy(speed.at[0, TOP:TOP + TR, 0:TC], u_out, store_sem.at[1]),
-        pltpu.make_async_copy(speed.at[1, TOP:TOP + TR, 0:TC], v_out, store_sem.at[2]),
-    ]
-    for cp in speed_stores:
-        cp.start()
-
-    cols_out = spread(TC, 128, 1, (128, TC), 0, True)
-    cols_out = jnp.concatenate([cols_out, cols_out], axis=0)
-    rows_out = spread(TR, WR, 0, (TR, WR), 8, False)
-    rows_out = jnp.concatenate([rows_out, rows_out], axis=1)
     wait_recv_all(copy_w)
     depth, wet = widen(cw, side_w, 2)
     inside = depth > 0.25
@@ -362,11 +369,29 @@
                    - FRICTION * flow_c * inv_depth + VISCOSITY * laplace(flow_c)),
         )
 
-    high, low = halves(jnp.concatenate([flow_a, flow_c], axis=0))
+    flow_out[0] = flow_a
+    flow_out[1] = flow_c
+    wait_send_all(fine_copy)
+    wait_send_all(copy_w)
+    wait_send_all(copy_s)
+
+
+def finish(s_ref, u_ref, v_ref, flow_ref, mask_ref, s_out, u_out, v_out, ca_out, cc_out, cur, store_sem):
+    stores = [
+        pltpu.make_async_copy(ref.at[TOP:TOP + TR, 0:TC], out, store_sem.at[k])
+        for k, (ref, out) in enumerate(((s_ref, s_out), (u_ref, u_out), (v_ref, v_out)))
+    ]
+    for cp in stores:
+        cp.start()
+    cols_out = spread(TC, 128, 1, (128, TC), 0, True)
+    cols_out = jnp.concatenate([cols_out, cols_out], axis=0)
+    rows_out = spread(TR, WR, 0, (TR, WR), 8, False)
+    rows_out = jnp.concatenate([rows_out, rows_out], axis=1)
+    high, low = halves(flow_ref[...].reshape(2 * WR, 128))
     wide = dot(jnp.concatenate([high, low], axis=1), cols_out)
     high, low = halves(jnp.concatenate([wide[0:WR], wide[WR:2 * WR]], axis=1))
     fine = dot(rows_out, jnp.concatenate([high, low], axis=0))
-    mask = ext[4, TOP:TOP + TR, 0:TC]
+    mask = mask_ref[...]
     cur[0] = fine[:, 0:TC] * mask
     cur[1] = fine[:, TC:2 * TC] * mask
     last = [
@@ -375,35 +400,31 @@
     ]
     for cp in last:
         cp.start()
-    surface_store.wait()
-    for cp in speed_stores:
-        cp.wait()
-    wait_send_all(fine_copy)
-    wait_send_all(copy_w)
-    wait_send_all(copy_s)
-    for cp in last:
+    for cp in stores + last:
         cp.wait()
 
 
 def solution(mesh):
     mesh_rows, mesh_cols = mesh.shape["along"], mesh.shape["cross"]
-    hbm = pl.BlockSpec(memory_space=pl.ANY)
+    hbm = pl.BlockSpec(memory_space=pltpu.HBM)
     vmem = pl.BlockSpec(memory_space=pltpu.VMEM)
 
+    def shape(*dims):
+        return jax.ShapeDtypeStruct(dims, F32)
+
     def per_device(surface, along_speed, cross_speed, water_depth, wet_mask, ship_cells, ship_pressure):
-        tile = jax.ShapeDtypeStruct((TR, TC), F32)
-        sems = [pltpu.SemaphoreType.DMA((8,))] * 6
-        return pl.pallas_call(
+        ships = ship_pressure.shape[0]
+        state = pl.pallas_call(
             functools.partial(kernel, mesh_rows, mesh_cols),
-            out_shape=[tile] * 5,
-            in_specs=[hbm] * 5 + [vmem] * 2,
-            out_specs=[hbm] * 5,
+            out_shape=[shape(ER, EC)] * 3 + [shape(2, WR, 128), shape(TR, TC)],
+            in_specs=[hbm] * 7,
+            out_specs=[vmem] * 5,
             scratch_shapes=[
                 pltpu.VMEM((5, ER, EC), F32),
-                pltpu.VMEM((2, ER, EC), F32),
                 pltpu.VMEM((TR, TC), jnp.int32),
+                pltpu.VMEM((STEPS, ships), jnp.int32),
+                pltpu.VMEM((1, ships), F32),
                 pltpu.VMEM((STEPS, ER, EC), F32),
-                pltpu.VMEM((ER, EC), F32),
                 pltpu.VMEM((ER, EC), F32),
                 pltpu.VMEM((ER, EC), F32),
                 pltpu.VMEM((10, TR, 128), F32),
@@ -417,14 +438,21 @@
                 pltpu.VMEM((3, 128, 128), F32),
                 pltpu.VMEM((2, WR, 128), F32),
                 pltpu.VMEM((3, WR, 128), F32),
-                pltpu.VMEM((2, TR, TC), F32),
-                pltpu.SemaphoreType.DMA((5,)),
-                pltpu.SemaphoreType.DMA((5,)),
-            ] + sems,
+                pltpu.SemaphoreType.DMA((7,)),
+            ] + [pltpu.SemaphoreType.DMA((8,))] * 6,
             compiler_params=pltpu.CompilerParams(
                 collective_id=0, has_side_effects=True, vmem_limit_bytes=32 * 1024 * 1024),
-        )(surface, along_speed, cross_speed, water_depth, wet_mask, ship_cells,
-          ship_pressure.reshape(1, ship_pressure.shape[0]))
+        )(*(pltpu.with_memory_space_constraint(x, pltpu.HBM) for x in (
+            surface, along_speed, cross_speed, water_depth, wet_mask, ship_cells,
+            ship_pressure.reshape(1, ships))))
+        return pl.pallas_call(
+            finish,
+            out_shape=[shape(TR, TC)] * 5,
+            in_specs=[vmem] * 5,
+            out_specs=[hbm] * 5,
+            scratch_shapes=[pltpu.VMEM((2, TR, TC), F32), pltpu.SemaphoreType.DMA((5,))],
+            compiler_params=pltpu.CompilerParams(vmem_limit_bytes=16 * 1024 * 1024),
+        )(*state)
 
     tiled = P("along", "cross")
     return jax.shard_map(

time: 38.7 us -> 29.9 us (0.77)
  local copies, waits for them, and re-layouts: 8.47 us -> 0 us
    unnamed x19 -> x0, local copies, waits for them, and re-layouts: 8.47 us -> none
    pallas_call x1, Pallas kernels: 29.3 us -> 28.1 us  [per_device(): pl.pallas_call(functools.partial(kernel, mesh_rows, mesh_cols), out_shape...]
    pallas_call x0 -> x1, Pallas kernels: none -> 1.11 us  [per_device(): pl.pallas_call(finish, out_shape=[shape(TR, TC)] * 5, in_specs=[vmem] * 5...]
where the time goes in v2:
time: 29.9 us; the launch traced here: 29.8 us
  Pallas kernels  29.2 us (98%)
  between operations  0.64 us (2%)
    pallas_call x1, Pallas kernels, per_device(): pl.pallas_call(functools.partial(kernel, mesh_rows, mesh_cols), out_shape...  28.1 us
    pallas_call x1, Pallas kernels, per_device(): pl.pallas_call(finish, out_shape=[shape(TR, TC)] * 5, in_specs=[vmem] * 5...  1.11 us

profile of v2, /device:TPU:22, one launch (start us, length us, event | category | flops | bytes accessed | tf_op | source)
XLA Modules:
  0.0 29.8 jit_solution(14370484333680702905)
XLA Ops:
  0.6 28.1 %shard_map.110 = (f32[160,384]{1,0:T(8,128)S(1)}, f32[160,384]{1,0:T(8,128)S(1)}, f32[160,384]{1,0:T(8,128)S(1)}, f32[2,48,128]{2,1,0:T(8,128)S(1)}, f32[128,256]{1,0:T(8,128)S(1)}) custom-call(f32[128,256]{1,0:T(8,128)} %s_in.1, f32[128,256]{1,0:T(8,128)} %u_in.1, f32[128,256]{1,0:T(8,128)} %v_in.1, f32[128,256]{1,0:T(8,128)} %d_in.1, s32[128,256]{1,0:T(8,128)} %w_in.1, ...), custom_call_target="tpu_custom_call" | custom-call | tf_op jit(solution)/shard_map/pallas_call | solution.py:417
  28.7 1.1 %shard_map.111 = (f32[128,256]{1,0:T(8,128)}, f32[128,256]{1,0:T(8,128)}, f32[128,256]{1,0:T(8,128)}, f32[128,256]{1,0:T(8,128)}, f32[128,256]{1,0:T(8,128)}) custom-call(f32[160,384]{1,0:T(8,128)S(1)} %get-tuple-element.10.s_ref, f32[160,384]{1,0:T(8,128)S(1)} %get-tuple-element.11.u_ref, f32[160,384]{1,0:T(8,128)S(1)} %get-tuple-element.12.v_ref, ...), custom_call_target="tpu_custom_call" | custom-call | tf_op jit(solution)/shard_map/pallas_call | solution.py:448

commit v3 on v2

v3 whole, which is shorter than its diff:
```python
import functools

import jax
import jax.numpy as jnp
from jax import lax
from jax.experimental import pallas as pl
from jax.experimental.pallas import tpu as pltpu
from jax.sharding import PartitionSpec as P

STEPS = 2
CIRC = 3
CONTINUITY = 0.25
MOMENTUM = 0.3
POTENTIAL = 0.5
CIRC_LEVEL = 0.2
CIRC_FORCE = 0.3
FRICTION = 0.1
VISCOSITY = 0.1

MESH = pl.DeviceIdType.MESH
F32 = jnp.float32
BF16 = jnp.bfloat16

TR = 128
TC = 256
TOP = 16
ER = TR + 2 * TOP
EC = 128
SIDE = 58
CR = TR // 4
CC = TC // 4
WR = CR + 16
CHUNK = 32
OWN = [(r, CHUNK) for r in range(TOP, TOP + TR, CHUNK)]
ALL = [(TOP - 8, 8)] + OWN + [(TOP + TR, 8)]
CROSS = [(0, -1), (0, 1)]
ALONG = [(-1, 0), (1, 0)]
DIRS = CROSS + [(-1, -1), (-1, 1), (1, -1), (1, 1)] + ALONG
HALO = 6


def iota(shape, dim):
    return lax.broadcasted_iota(jnp.int32, shape, dim)


def halves(x):
    high = x.astype(BF16)
    return high, (x - high.astype(F32)).astype(BF16)


def dot(x, y):
    return jnp.dot(x, y, preferred_element_type=F32)


def dot_nt(x, y):
    return lax.dot_general(x, y, (((1,), (1,)), ((), ())), preferred_element_type=F32)


def row_next(x, keep):
    return pltpu.roll(x, x.shape[0] - 1, 0)[keep]


def row_prev(x, keep):
    return pltpu.roll(x, 1, 0)[keep]


def col_next(x):
    return pltpu.roll(x, x.shape[1] - 1, 1)


def col_prev(x):
    return pltpu.roll(x, 1, 1)


def slant(x, step):
    row = iota(x.shape, 0)
    for bit in (1, 2, 4):
        if step * bit % 128:
            x = jnp.where((row & bit) != 0, pltpu.roll(x, step * bit % 128, 1), x)
    return x


def spread(fine, coarse, fine_dim, shape, first, wrap):
    f = iota(shape, fine_dim)
    c = iota(shape, 1 - fine_dim)
    base = lax.shift_right_logical(f, 2) + first
    k = f & 3
    weight = jnp.where((k == 0) | (k == 3), 0.375, 0.125)
    other = base + jnp.where(k < 2, -1, 1)
    if wrap:
        other = other & (coarse - 1)
    zero = jnp.zeros(shape, F32)
    return (jnp.where(c == base, 1.0 - weight, zero) + jnp.where(c == other, weight, zero)).astype(BF16)


def kernel(
    mesh_rows, mesh_cols,
    s_in, u_in, v_in, d_in, w_in, cells_in, press_in,
    s_out, u_out, v_out, flow_out, mask_out,
    ext, wraw, cells_ref, press_ref, forc, r1, curv, planes,
    e_ext, e_forc, e_r1, e_s, e_u, e_v, e_curv, e_planes,
    packt, got, corner_send, corner, corner_s_send, corner_s,
    ts_w, ts_s, side_w, side_s, cw, cs,
    load_sem, f_send, f_recv, w_send, w_recv, c_send, c_recv,
):
    a = lax.axis_index("along")
    c = lax.axis_index("cross")
    total_cols = TC * mesh_cols

    def there(da, dc):
        ok = None
        for cond in ([a > 0] if da < 0 else [a < mesh_rows - 1] if da > 0 else []) + (
            [c > 0] if dc < 0 else [c < mesh_cols - 1] if dc > 0 else []
        ):
            ok = cond if ok is None else ok & cond
        return ok

    def device(da, dc):
        return (a + da, c + dc)

    barrier = pltpu.get_barrier_semaphore()
    for da, dc in DIRS:
        @pl.when(there(da, dc))
        def _(da=da, dc=dc):
            pl.semaphore_signal(barrier, inc=1, device_id=device(da, dc), device_id_type=MESH)

    loads = []
    for k, src in enumerate((s_in, u_in, v_in, d_in)):
        loads.append(pltpu.make_async_copy(src, ext.at[k, TOP:TOP + TR, 0:TC], load_sem.at[k]))
    loads.append(pltpu.make_async_copy(w_in, wraw, load_sem.at[4]))
    loads.append(pltpu.make_async_copy(cells_in, cells_ref, load_sem.at[5]))
    loads.append(pltpu.make_async_copy(press_in, press_ref, load_sem.at[6]))
    for cp in loads:
        cp.start()

    for ref in (ext, e_ext):
        for f in range(5):
            ref[f, 0:8, :] = jnp.zeros((8, ref.shape[2]), F32)
            ref[f, ER - 8:ER, :] = jnp.zeros((8, ref.shape[2]), F32)
    for ref in (r1, s_out, u_out, v_out, curv, e_r1, e_s, e_u, e_v, e_curv):
        ref[0:8, :] = jnp.zeros((8, ref.shape[1]), F32)
        ref[ER - 8:ER, :] = jnp.zeros((8, ref.shape[1]), F32)
    for side in (side_w, side_s):
        side[0:CC] = jnp.zeros((CC, 128), F32)
        side[CC + 8:120] = jnp.zeros((112 - CC, 128), F32)
    for da, dc in DIRS:
        @pl.when(jnp.logical_not(there(da, dc)))
        def _(da=da, dc=dc):
            if dc == 0:
                at = TOP - 8 if da < 0 else TOP + TR
                for f in range(5):
                    ext[f, at:at + 8, 0:TC] = jnp.zeros((8, TC), F32)
                at = 0 if da < 0 else WR - 8
                for ref, nf in ((cw, 2), (cs, 3)):
                    for f in range(nf):
                        ref[f, at:at + 8] = jnp.zeros((8, 128), F32)
                return
            right = 1 if dc > 0 else 0
            if da == 0:
                got[32 * right:32 * right + 32] = jnp.zeros((32, 128), F32)
                at = CC if right else 120
                side_w[at:at + 8] = jnp.zeros((8, 128), F32)
                side_s[at:at + 8] = jnp.zeros((8, 128), F32)
            else:
                corner[0 if da < 0 else 1, right] = jnp.zeros((2, 128), F32)
                corner_s[0 if da < 0 else 1, right] = jnp.zeros((2, 128), F32)

    rows_near = 1 + jnp.where(a > 0, 1, 0) + jnp.where(a < mesh_rows - 1, 1, 0)
    cols_near = 1 + jnp.where(c > 0, 1, 0) + jnp.where(c < mesh_cols - 1, 1, 0)
    for cp in loads:
        cp.wait()
    own_wet = wraw[...].astype(F32)
    ext[4, TOP:TOP + TR, 0:TC] = own_wet
    mask_out[...] = own_wet

    lane = iota((TR, 128), 1)
    packed = jnp.zeros((TR, 128), F32)
    for f in range(5):
        for part, start, move in ((1, HALO * f, HALO * f + HALO), (0, 32 + HALO * f, 32 + HALO * f)):
            edge = pltpu.roll(ext[f, TOP:TOP + TR, 128 * part:128 * part + 128], move, 1)
            packed = jnp.where((lane >= start) & (lane < start + HALO), edge, packed)
    packt[...] = packed.T
    for t in range(2):
        rows = packed[0:8] if t == 0 else packed[TR - 8:TR]
        for side in range(2):
            block = rows if side == 0 else pltpu.roll(rows, 96, 1)
            block = jnp.where(lane[0:8] < 32, block, 0.0)
            block = slant(block, 32)
            corner_send[t, side, 0:1] = jnp.sum(block[0:4], axis=0, keepdims=True)
            corner_send[t, side, 1:2] = jnp.sum(block[4:8], axis=0, keepdims=True)

    def fine_copy(n):
        da, dc = DIRS[n]
        if da == 0:
            at = 0 if dc > 0 else 32
            src, dst = packt.at[at:at + 32], got.at[at:at + 32]
        elif dc == 0:
            src = ext.at[:, TOP:TOP + 8, 0:TC] if da < 0 else ext.at[:, TOP + TR - 8:TOP + TR, 0:TC]
            dst = ext.at[:, TOP + TR:TOP + TR + 8, 0:TC] if da < 0 else ext.at[:, TOP - 8:TOP, 0:TC]
        else:
            side = 0 if dc > 0 else 1
            src = corner_send.at[0 if da < 0 else 1, side]
            dst = corner.at[1 if da < 0 else 0, side]
        return pltpu.make_async_remote_copy(
            src_ref=src, dst_ref=dst, send_sem=f_send.at[n], recv_sem=f_recv.at[n],
            device_id=device(da, dc), device_id_type=MESH)

    def coarse_copy(ts, side, field, send, recv):
        def make(n):
            da, dc = DIRS[n]
            if dc == 0:
                src = field.at[:, 8:16] if da < 0 else field.at[:, CR:CR + 8]
                dst = field.at[:, CR + 8:CR + 16] if da < 0 else field.at[:, 0:8]
            elif da == 0:
                at = CC if dc < 0 else 120
                src = ts.at[0 if dc < 0 else 1]
                dst = side.at[at:at + 8]
            else:
                src = corner_s_send.at[0 if da < 0 else 1, 0 if dc > 0 else 1]
                dst = corner_s.at[1 if da < 0 else 0, 0 if dc > 0 else 1]
            return pltpu.make_async_remote_copy(
                src_ref=src, dst_ref=dst, send_sem=send.at[n], recv_sem=recv.at[n],
                device_id=device(da, dc), device_id_type=MESH)
        return make

    def start_all(make, chosen=DIRS):
        for da, dc in chosen:
            n = DIRS.index((da, dc))
            @pl.when(there(da, dc))
            def _(n=n):
                make(n).start()

    def wait_recv_all(make, chosen=DIRS):
        for da, dc in chosen:
            n = DIRS.index((da, dc))
            @pl.when(there(-da, -dc))
            def _(n=n):
                make(n).wait_recv()

    def wait_send_all(make, chosen=DIRS):
        for da, dc in chosen:
            n = DIRS.index((da, dc))
            @pl.when(there(da, dc))
            def _(n=n):
                make(n).wait_send()

    pl.semaphore_wait(barrier, rows_near * cols_near - 1)
    copy_w = coarse_copy(ts_w, side_w, cw, w_send, w_recv)
    copy_s = coarse_copy(ts_s, side_s, cs, c_send, c_recv)
    start_all(fine_copy)

    def pool_matrix(width, wanted, shift, split):
        col = iota((width, 128), 0)
        col = jnp.where(col < split, col - shift[0], col - shift[1])
        to = iota((width, 128), 1)
        hit = (lax.shift_right_arithmetic(col, 2) == to) & wanted(to) & (to < CC)
        one = jnp.where(hit, 1.0, 0.0).astype(BF16)
        return jnp.concatenate([one, one], axis=0)

    def edge_matrix(width, shift, split):
        to = iota((16, width), 0)
        to = jnp.where(to < 8, to, to + (CC - 16))
        col = iota((16, width), 1)
        col = jnp.where(col < split, col - shift[0], col - shift[1])
        one = jnp.where(lax.shift_right_arithmetic(col, 2) == to, 1.0, 0.0).astype(BF16)
        return jnp.concatenate([one, one], axis=1)

    def row_means(ref, first, nf, nh, scale):
        tall = []
        for f in range(nf):
            wide = []
            for h in range(nh):
                n = nh * (first + f) + h
                total = ref[n, pl.ds(0, CR, stride=4), :]
                for k in range(1, 4):
                    total = total + ref[n, pl.ds(k, CR, stride=4), :]
                wide.append(total * scale)
            tall.append(jnp.concatenate(wide, axis=1) if nh > 1 else wide[0])
        tall.append(jnp.zeros((TR - nf * CR, 128 * nh), F32))
        return jnp.concatenate(halves(jnp.concatenate(tall, axis=0)), axis=1)

    own = (0, 0)
    sides = (HALO, 128 - HALO - TC)
    pool_all = pool_matrix(TC, lambda j: j >= 0, own, TC)
    pool_mid = pool_matrix(TC, lambda j: (j >= 8) & (j < CC - 8), own, TC)
    pool_side = pool_matrix(EC, lambda j: (j < 8) | (j >= CC - 8), sides, EC // 2)
    edge_all = edge_matrix(TC, own, TC)
    edge_side = edge_matrix(EC, sides, EC // 2)

    for h in range(2):
        planes[6 + h] = ext[3, TOP:TOP + TR, 128 * h:128 * h + 128]
        planes[8 + h] = ext[4, TOP:TOP + TR, 128 * h:128 * h + 128]
    means = row_means(planes, 3, 2, 2, 1.0 / 16.0)
    edges = dot_nt(edge_all, means)
    ts_w[0] = edges[0:8]
    ts_w[1] = edges[8:16]
    coarse = dot(means, pool_all)
    for f in range(2):
        cw[f, 8:8 + CR] = coarse[f * CR:(f + 1) * CR]
    start_all(copy_w, CROSS)

    ext_row = a * TR - TOP + iota((ER, 8), 0)
    own_col = c * TC + iota((TC, 8), 0)
    side_col = iota((EC, 8), 0)
    side_col = c * TC + jnp.where(side_col < EC // 2, side_col - sides[0], side_col - sides[1])
    for step in range(STEPS):
        cells = cells_ref[step:step + 1, :]
        row_hit = jnp.where(ext_row == lax.div(cells, total_cols), press_ref[...], 0.0)
        for ref, col in ((forc, own_col), (e_forc, side_col)):
            col_hit = jnp.where(col == lax.rem(cells, total_cols), 1.0, 0.0)
            ref[step] = lax.dot_general(
                row_hit, col_hit, (((1,), (1,)), ((), ())),
                precision=lax.Precision.HIGHEST, preferred_element_type=F32)

    def waves(base, force, first, last, bend, u_ref, v_ref, stress_ref, nh):
        surface, along, cross = base.at[0], base.at[1], base.at[2]
        for step in range(STEPS):
            raised = first if step == 0 else last
            for r, n in ALL:
                keep = slice(8, 8 + n)
                wide = slice(r - 8, r + n + 8)
                here = slice(r, r + n)
                depth = base[3, wide, :]
                du = depth * along[wide, :]
                dv = depth[keep] * cross[here, :]
                flux = (row_next(du, keep) - row_prev(du, keep)) + (col_next(dv) - col_prev(dv))
                raised[here, :] = base[4, here, :] * (
                    surface[here, :] - (0.5 * CONTINUITY) * flux + force[step, here, :])
            for r, n in ALL:
                keep = slice(8, 8 + n)
                x = raised[r - 8:r + n + 8, :]
                mid = x[keep]
                bend[r:r + n, :] = (
                    row_next(x, keep) + row_prev(x, keep) + col_next(mid) + col_prev(mid) - 4.0 * mid)
            for r, n in (ALL if step < STEPS - 1 else OWN):
                keep = slice(8, 8 + n)
                here = slice(r, r + n)
                x = raised[r - 8:r + n + 8, :]
                k = bend[r - 8:r + n + 8, :]
                depth = base[3, here, :]
                wet = base[4, here, :]
                disp = depth * depth * (1.0 / 3.0)
                push_a = (row_next(x, keep) - row_prev(x, keep)) + disp * (row_next(k, keep) - row_prev(k, keep))
                x = x[keep]
                k = k[keep]
                push_c = (col_next(x) - col_prev(x)) + disp * (col_next(k) - col_prev(k))
                u = wet * (along[here, :] - (0.5 * MOMENTUM) * push_a)
                v = wet * (cross[here, :] - (0.5 * MOMENTUM) * push_c)
                u_ref[here, :] = u
                v_ref[here, :] = v
                if (r, n) in OWN:
                    pot = POTENTIAL * x * x
                    stress = (depth * u * u + pot, depth * u * v, depth * v * v + pot)
                    at = slice(r - TOP, r - TOP + n)
                    for f in range(3):
                        for h in range(nh):
                            part = stress[f][:, 128 * h:128 * h + 128]
                            if step > 0:
                                part = part + stress_ref[nh * f + h, at]
                            stress_ref[nh * f + h, at] = part
            surface, along, cross = raised, u_ref, v_ref

    wait_recv_all(fine_copy, ALONG)
    waves(ext, forc, r1, s_out, curv, u_out, v_out, planes, 2)
    coarse_mid = dot(row_means(planes, 0, 3, 2, 1.0 / (16.0 * STEPS)), pool_mid)

    rows = slice(TOP - 8, TOP + TR + 8)
    halo_lane = iota((TR + 16, 128), 1)
    for f in range(5):
        left = pltpu.roll(ext[f, rows, 0:128], HALO, 1)
        right = pltpu.roll(ext[f, rows, 128:256], 128 - HALO, 1)
        e_ext[f, rows, :] = jnp.where(halo_lane < EC // 2, left, right)

    wait_recv_all(fine_copy, DIRS[:6])

    def open_corner(t):
        rows = jnp.zeros((8, 128), F32)
        for side in range(2):
            block = jnp.concatenate([
                jnp.broadcast_to(corner[t, side, 0:1], (4, 128)),
                jnp.broadcast_to(corner[t, side, 1:2], (4, 128))], axis=0)
            block = slant(pltpu.roll(block, 32, 1) if side else block, 96)
            rows = jnp.where(lax.shift_right_logical(lane[0:8], 5) == side, block, rows)
        return rows

    halo = jnp.concatenate([open_corner(0), got[...].T, open_corner(1)], axis=0)
    for f in range(5):
        left = pltpu.roll(halo, (128 - HALO * f) % 128, 1)
        right = pltpu.roll(halo, 128 - HALO - 32 - HALO * f, 1)
        e_ext[f, rows, :] = jnp.where(
            halo_lane < HALO, left, jnp.where(halo_lane >= 128 - HALO, right, e_ext[f, rows, :]))
    waves(e_ext, e_forc, e_r1, e_s, e_curv, e_u, e_v, e_planes, 1)

    means = row_means(e_planes, 0, 3, 1, 1.0 / (16.0 * STEPS))
    edges = dot_nt(edge_side, means)
    ts_s[0] = edges[0:8]
    ts_s[1] = edges[8:16]
    start_all(copy_s, CROSS)
    coarse = dot(means, pool_side)
    small = iota((8, 128), 1)
    for t in range(2):
        for side in range(2):
            at = 0 if side else CC - 8
            packed = [jnp.zeros((8, 128), F32)] * 2
            for f in range(3):
                r = f * CR + (0 if t == 0 else CR - 8)
                block = jnp.where((small >= at) & (small < at + 8), coarse[r:r + 8], 0.0)
                block = pltpu.roll(block, (128 - at + 64 * (f % 2)) % 128, 1, stride=8, stride_axis=0)
                packed[f // 2] = packed[f // 2] + block
            for k in range(2):
                corner_s_send[t, side, k:k + 1] = jnp.sum(packed[k], axis=0, keepdims=True)
    start_all(copy_s, DIRS[2:6])
    coarse = coarse + coarse_mid
    for f in range(3):
        cs[f, 8:8 + CR] = coarse[f * CR:(f + 1) * CR]
    start_all(copy_s, ALONG)

    rows = slice(TOP, TOP + TR)
    for ref, edge in ((s_out, e_s), (u_out, e_u), (v_out, e_v)):
        ref[rows, 0:128] = jnp.where(lane < 16, pltpu.roll(edge[rows], 128 - HALO, 1), ref[rows, 0:128])
        ref[rows, 128:256] = jnp.where(lane >= 112, pltpu.roll(edge[rows], HALO, 1), ref[rows, 128:256])

    wait_recv_all(copy_w, CROSS)
    mid = side_w[...].T
    for f in range(2):
        cw[f, 8:8 + CR] = cw[f, 8:8 + CR] + mid[f * CR:(f + 1) * CR]
    start_all(copy_w, ALONG)
    wait_recv_all(copy_w, ALONG)
    depth, wet = cw[0], cw[1]
    inside = depth > 0.25
    inv_depth = 1.0 / jnp.maximum(depth, 0.25)

    wait_recv_all(copy_s)
    mid = side_s[...].T
    wide = []
    for f in range(3):
        ends = []
        for t in range(2):
            rows = cs[f, 0:8] if t == 0 else cs[f, WR - 8:WR]
            for side in range(2):
                at = CC if side else 120
                block = jnp.broadcast_to(corner_s[t, side, f // 2:f // 2 + 1], (8, 128))
                block = slant(pltpu.roll(block, (at - 64 * (f % 2)) % 128, 1), 120)
                rows = rows + jnp.where((small >= at) & (small < at + 8), block, 0.0)
            ends.append(rows)
        wide.append(jnp.concatenate(
            [ends[0], cs[f, 8:8 + CR] + mid[f * CR:(f + 1) * CR], ends[1]], axis=0))
    s0, s1, s2 = wide

    def dr(x):
        return 0.5 * (pltpu.roll(x, WR - 1, 0) - pltpu.roll(x, 1, 0))

    def dc(x):
        return 0.5 * (col_next(x) - col_prev(x))

    def laplace(x):
        return pltpu.roll(x, WR - 1, 0) + pltpu.roll(x, 1, 0) + col_next(x) + col_prev(x) - 4.0 * x

    force_a = -(dr(s0) + dc(s1)) * inv_depth
    force_c = -(dr(s1) + dc(s2)) * inv_depth
    flow_a = wet * (CIRC_FORCE * force_a)
    flow_c = wet * (CIRC_FORCE * force_c)
    elevation = jnp.zeros_like(depth)
    for _ in range(CIRC - 1):
        level = elevation - CIRC_LEVEL * (dr(depth * flow_a) + dc(depth * flow_c))
        elevation = jnp.where(inside, level, 0.0)
        flow_a, flow_c = (
            wet * (flow_a + CIRC_FORCE * (force_a - dr(elevation))
                   - FRICTION * flow_a * inv_depth + VISCOSITY * laplace(flow_a)),
            wet * (flow_c + CIRC_FORCE * (force_c - dc(elevation))
                   - FRICTION * flow_c * inv_depth + VISCOSITY * laplace(flow_c)),
        )

    flow_out[0] = flow_a
    flow_out[1] = flow_c
    wait_send_all(fine_copy)
    wait_send_all(copy_w, CROSS + ALONG)
    wait_send_all(copy_s)


def finish(s_ref, u_ref, v_ref, flow_ref, mask_ref, s_out, u_out, v_out, ca_out, cc_out, cur, store_sem):
    stores = [
        pltpu.make_async_copy(ref.at[TOP:TOP + TR, 0:TC], out, store_sem.at[k])
        for k, (ref, out) in enumerate(((s_ref, s_out), (u_ref, u_out), (v_ref, v_out)))
    ]
    for cp in stores:
        cp.start()
    cols_out = spread(TC, 128, 1, (128, TC), 0, True)
    cols_out = jnp.concatenate([cols_out, cols_out], axis=0)
    rows_out = spread(TR, WR, 0, (TR, WR), 8, False)
    rows_out = jnp.concatenate([rows_out, rows_out], axis=1)
    high, low = halves(flow_ref[...].reshape(2 * WR, 128))
    wide = dot(jnp.concatenate([high, low], axis=1), cols_out)
    high, low = halves(jnp.concatenate([wide[0:WR], wide[WR:2 * WR]], axis=1))
    fine = dot(rows_out, jnp.concatenate([high, low], axis=0))
    mask = mask_ref[...]
    cur[0] = fine[:, 0:TC] * mask
    cur[1] = fine[:, TC:2 * TC] * mask
    last = [
        pltpu.make_async_copy(cur.at[0], ca_out, store_sem.at[3]),
        pltpu.make_async_copy(cur.at[1], cc_out, store_sem.at[4]),
    ]
    for cp in last:
        cp.start()
    for cp in stores + last:
        cp.wait()


def solution(mesh):
    mesh_rows, mesh_cols = mesh.shape["along"], mesh.shape["cross"]
    hbm = pl.BlockSpec(memory_space=pltpu.HBM)
    vmem = pl.BlockSpec(memory_space=pltpu.VMEM)

    def shape(*dims):
        return jax.ShapeDtypeStruct(dims, F32)

    def per_device(surface, along_speed, cross_speed, water_depth, wet_mask, ship_cells, ship_pressure):
        ships = ship_pressure.shape[0]
        state = pl.pallas_call(
            functools.partial(kernel, mesh_rows, mesh_cols),
            out_shape=[shape(ER, TC)] * 3 + [shape(2, WR, 128), shape(TR, TC)],
            in_specs=[hbm] * 7,
            out_specs=[vmem] * 5,
            scratch_shapes=[
                pltpu.VMEM((5, ER, TC), F32),
                pltpu.VMEM((TR, TC), jnp.int32),
                pltpu.VMEM((STEPS, ships), jnp.int32),
                pltpu.VMEM((1, ships), F32),
                pltpu.VMEM((STEPS, ER, TC), F32),
                pltpu.VMEM((ER, TC), F32),
                pltpu.VMEM((ER, TC), F32),
                pltpu.VMEM((10, TR, 128), F32),
                pltpu.VMEM((5, ER, EC), F32),
                pltpu.VMEM((STEPS, ER, EC), F32),
            ] + [pltpu.VMEM((ER, EC), F32)] * 5 + [
                pltpu.VMEM((3, TR, 128), F32),
                pltpu.VMEM((128, 128), F32),
                pltpu.VMEM((128, 128), F32),
            ] + [pltpu.VMEM((2, 2, 2, 128), F32)] * 4 + [
                pltpu.VMEM((2, 8, 128), F32),
                pltpu.VMEM((2, 8, 128), F32),
                pltpu.VMEM((128, 128), F32),
                pltpu.VMEM((128, 128), F32),
                pltpu.VMEM((2, WR, 128), F32),
                pltpu.VMEM((3, WR, 128), F32),
                pltpu.SemaphoreType.DMA((7,)),
            ] + [pltpu.SemaphoreType.DMA((8,))] * 6,
            compiler_params=pltpu.CompilerParams(
                collective_id=0, has_side_effects=True, vmem_limit_bytes=32 * 1024 * 1024),
        )(*(pltpu.with_memory_space_constraint(x, pltpu.HBM) for x in (
            surface, along_speed, cross_speed, water_depth, wet_mask, ship_cells,
            ship_pressure.reshape(1, ships))))
        return pl.pallas_call(
            finish,
            out_shape=[shape(TR, TC)] * 5,
            in_specs=[vmem] * 5,
            out_specs=[hbm] * 5,
            scratch_shapes=[pltpu.VMEM((2, TR, TC), F32), pltpu.SemaphoreType.DMA((5,))],
            compiler_params=pltpu.CompilerParams(vmem_limit_bytes=16 * 1024 * 1024),
        )(*state)

    tiled = P("along", "cross")
    return jax.shard_map(
        per_device,
        mesh=mesh,
        in_specs=(tiled,) * 5 + (P(), P()),
        out_specs=(tiled,) * 5,
        check_vma=False,
    )
```

time: 29.9 us -> 28.8 us (0.963)
  the two profiles are of different devices: /device:TPU:22 before, /device:TPU:8 now
where the time goes in v3:
time: 28.8 us; the launch traced here: 28.7 us
  Pallas kernels  28 us (97%)
  between operations  0.64 us (2%)
    pallas_call x1, Pallas kernels, per_device(): pl.pallas_call(functools.partial(kernel, mesh_rows, mesh_cols), out_shape...  26.9 us
    pallas_call x1, Pallas kernels, per_device(): pl.pallas_call(finish, out_shape=[shape(TR, TC)] * 5, in_specs=[vmem] * 5...  1.11 us

profile of v3, /device:TPU:8, one launch (start us, length us, event | category | flops | bytes accessed | tf_op | source)
XLA Modules:
  0.0 28.7 jit_solution(5660102973228035382)
XLA Ops:
  0.6 26.9 %shard_map.110 = (f32[160,256]{1,0:T(8,128)S(1)}, f32[160,256]{1,0:T(8,128)S(1)}, f32[160,256]{1,0:T(8,128)S(1)}, f32[2,48,128]{2,1,0:T(8,128)S(1)}, f32[128,256]{1,0:T(8,128)S(1)}) custom-call(f32[128,256]{1,0:T(8,128)} %s_in.1, f32[128,256]{1,0:T(8,128)} %u_in.1, f32[128,256]{1,0:T(8,128)} %v_in.1, f32[128,256]{1,0:T(8,128)} %d_in.1, s32[128,256]{1,0:T(8,128)} %w_in.1, ...), custom_call_target="tpu_custom_call" | custom-call | tf_op jit(solution)/shard_map/pallas_call | solution.py:519
  27.6 1.1 %shard_map.111 = (f32[128,256]{1,0:T(8,128)}, f32[128,256]{1,0:T(8,128)}, f32[128,256]{1,0:T(8,128)}, f32[128,256]{1,0:T(8,128)}, f32[128,256]{1,0:T(8,128)}) custom-call(f32[160,256]{1,0:T(8,128)S(1)} %get-tuple-element.10.s_ref, f32[160,256]{1,0:T(8,128)S(1)} %get-tuple-element.11.u_ref, f32[160,256]{1,0:T(8,128)S(1)} %get-tuple-element.12.v_ref, ...), custom_call_target="tpu_custom_call" | custom-call | tf_op jit(solution)/shard_map/pallas_call | solution.py:553

commit v4 on v3

--- a/solution.py
+++ b/solution.py
@@ -37,6 +37,9 @@
 ALONG = [(-1, 0), (1, 0)]
 DIRS = CROSS + [(-1, -1), (-1, 1), (1, -1), (1, 1)] + ALONG
 HALO = 6
+E_BOTH = [(TOP - 8, TR // 2 + 8), (TOP + TR // 2, TR // 2 + 8)]
+E_OWN = [(TOP, TR // 2), (TOP + TR // 2, TR // 2)]
+E_ALL = [(TOP - 8, 8)] + E_OWN + [(TOP + TR, 8)]
 
 
 def iota(shape, dim):
@@ -96,9 +99,9 @@
 def kernel(
     mesh_rows, mesh_cols,
     s_in, u_in, v_in, d_in, w_in, cells_in, press_in,
-    s_out, u_out, v_out, flow_out, mask_out,
-    ext, wraw, cells_ref, press_ref, forc, r1, curv, planes,
-    e_ext, e_forc, e_r1, e_s, e_u, e_v, e_curv, e_planes,
+    s_out, u_out, v_out, flow_out, mask_out, cols_out, rows_out,
+    ext, wraw, cells_ref, press_ref, forc, r1, curv, slope, planes,
+    e_ext, e_forc, e_r1, e_s, e_u, e_v, e_curv, e_du, e_slope, e_planes,
     packt, got, corner_send, corner, corner_s_send, corner_s,
     ts_w, ts_s, side_w, side_s, cw, cs,
     load_sem, f_send, f_recv, w_send, w_recv, c_send, c_recv,
@@ -183,8 +186,7 @@
     for t in range(2):
         rows = packed[0:8] if t == 0 else packed[TR - 8:TR]
         for side in range(2):
-            block = rows if side == 0 else pltpu.roll(rows, 96, 1)
-            block = jnp.where(lane[0:8] < 32, block, 0.0)
+            block = jnp.where(lax.shift_right_logical(lane[0:8], 5) == side, rows, 0.0)
             block = slant(block, 32)
             corner_send[t, side, 0:1] = jnp.sum(block[0:4], axis=0, keepdims=True)
             corner_send[t, side, 1:2] = jnp.sum(block[4:8], axis=0, keepdims=True)
@@ -247,7 +249,7 @@
     pl.semaphore_wait(barrier, rows_near * cols_near - 1)
     copy_w = coarse_copy(ts_w, side_w, cw, w_send, w_recv)
     copy_s = coarse_copy(ts_s, side_s, cs, c_send, c_recv)
-    start_all(fine_copy)
+    start_all(fine_copy, DIRS[2:6] + CROSS + ALONG)
 
     def pool_matrix(width, wanted, shift, split):
         col = iota((width, 128), 0)
@@ -312,7 +314,9 @@
                 row_hit, col_hit, (((1,), (1,)), ((), ())),
                 precision=lax.Precision.HIGHEST, preferred_element_type=F32)
 
-    def waves(base, force, first, last, bend, u_ref, v_ref, stress_ref, nh):
+    def own_waves():
+        base, force, first, last, bend = ext, forc, r1, s_out, curv
+        u_ref, v_ref, stress_ref, nh = u_out, v_out, planes, 2
         surface, along, cross = base.at[0], base.at[1], base.at[2]
         for step in range(STEPS):
             raised = first if step == 0 else last
@@ -330,20 +334,21 @@
                 keep = slice(8, 8 + n)
                 x = raised[r - 8:r + n + 8, :]
                 mid = x[keep]
-                bend[r:r + n, :] = (
-                    row_next(x, keep) + row_prev(x, keep) + col_next(mid) + col_prev(mid) - 4.0 * mid)
+                down, up, right, left = row_next(x, keep), row_prev(x, keep), col_next(mid), col_prev(mid)
+                slope[0, r:r + n, :] = down - up
+                slope[1, r:r + n, :] = right - left
+                bend[r:r + n, :] = down + up + right + left - 4.0 * mid
             for r, n in (ALL if step < STEPS - 1 else OWN):
                 keep = slice(8, 8 + n)
                 here = slice(r, r + n)
-                x = raised[r - 8:r + n + 8, :]
+                x = raised[here, :]
                 k = bend[r - 8:r + n + 8, :]
                 depth = base[3, here, :]
                 wet = base[4, here, :]
                 disp = depth * depth * (1.0 / 3.0)
-                push_a = (row_next(x, keep) - row_prev(x, keep)) + disp * (row_next(k, keep) - row_prev(k, keep))
-                x = x[keep]
+                push_a = slope[0, here, :] + disp * (row_next(k, keep) - row_prev(k, keep))
                 k = k[keep]
-                push_c = (col_next(x) - col_prev(x)) + disp * (col_next(k) - col_prev(k))
+                push_c = slope[1, here, :] + disp * (col_next(k) - col_prev(k))
                 u = wet * (along[here, :] - (0.5 * MOMENTUM) * push_a)
                 v = wet * (cross[here, :] - (0.5 * MOMENTUM) * push_c)
                 u_ref[here, :] = u
@@ -360,57 +365,136 @@
                             stress_ref[nh * f + h, at] = part
             surface, along, cross = raised, u_ref, v_ref
 
+    def edge_waves():
+        surface, along, cross = e_ext.at[0], e_ext.at[1], e_ext.at[2]
+        for step in range(STEPS):
+            raised = e_r1 if step == 0 else e_s
+            e_du[...] = e_ext[3] * along[...]
+            for r, n in E_BOTH:
+                here, down, up = slice(r, r + n), slice(r + 1, r + n + 1), slice(r - 1, r + n - 1)
+                dv = e_ext[3, here, :] * cross[here, :]
+                flux = (e_du[down, :] - e_du[up, :]) + (col_next(dv) - col_prev(dv))
+                raised[here, :] = e_ext[4, here, :] * (
+                    surface[here, :] - (0.5 * CONTINUITY) * flux + e_forc[step, here, :])
+            for r, n in E_BOTH:
+                here, down, up = slice(r, r + n), slice(r + 1, r + n + 1), slice(r - 1, r + n - 1)
+                mid = raised[here, :]
+                right, left = col_next(mid), col_prev(mid)
+                e_slope[here, :] = right - left
+                e_curv[here, :] = raised[down, :] + raised[up, :] + right + left - 4.0 * mid
+            for r, n in (E_ALL if step < STEPS - 1 else E_OWN):
+                here, down, up = slice(r, r + n), slice(r + 1, r + n + 1), slice(r - 1, r + n - 1)
+                depth = e_ext[3, here, :]
+                wet = e_ext[4, here, :]
+                disp = depth * depth * (1.0 / 3.0)
+                k = e_curv[here, :]
+                push_a = (raised[down, :] - raised[up, :]) + disp * (e_curv[down, :] - e_curv[up, :])
+                push_c = e_slope[here, :] + disp * (col_next(k) - col_prev(k))
+                u = wet * (along[here, :] - (0.5 * MOMENTUM) * push_a)
+                v = wet * (cross[here, :] - (0.5 * MOMENTUM) * push_c)
+                e_u[here, :] = u
+                e_v[here, :] = v
+                if (r, n) in E_OWN:
+                    x = raised[here, :]
+                    pot = POTENTIAL * x * x
+                    at = slice(r - TOP, r - TOP + n)
+                    for f, part in enumerate((depth * u * u + pot, depth * u * v, depth * v * v + pot)):
+                        e_planes[f, at] = part + e_planes[f, at] if step > 0 else part
+            surface, along, cross = raised, e_u, e_v
+
+    def corner_matrix(side):
+        lane_of = iota((EC, 128), 0)
+        to = (iota((EC, 128), 1) & 7) * 4 + (HALO if side else 128 - HALO - 32)
+        one = jnp.where((lane_of >= to) & (lane_of < to + 4), 1.0, 0.0).astype(BF16)
+        return jnp.concatenate([one, one], axis=0)
+
+    pool_corner = jnp.concatenate([corner_matrix(0), corner_matrix(1)], axis=1)
+
+    def open_matrix(at):
+        lane_of = iota((128, 128), 0)
+        to = iota((128, 128), 1)
+        one = jnp.where((to >= at) & (to < at + 8) & ((lane_of & 7) == to - at), 1.0, 0.0).astype(BF16)
+        return jnp.concatenate([one, one], axis=0)
+
+    open_corners = jnp.concatenate([open_matrix(120), open_matrix(CC)], axis=0)
+
+    def fill_edge(r, n):
+        at = iota((n, 128), 1)
+        for f in range(5):
+            left = pltpu.roll(ext[f, r:r + n, 0:128], HALO, 1)
+            right = pltpu.roll(ext[f, r:r + n, 128:256], 128 - HALO, 1)
+            both = jnp.where(at < EC // 2, left, right)
+            e_ext[f, r:r + n, :] = jnp.where((at >= HALO) & (at < 128 - HALO), both, 0.0)
+
+    fill_edge(TOP, TR)
+
+    n_lane = iota((192, 5 * 128), 0)
+    to = iota((192, 5 * 128), 1)
+    to_field, to_lane = lax.shift_right_logical(to, 7), to & 127
+    from_lane = HALO * to_field + jnp.where(to_lane < HALO, to_lane, to_lane - (128 - HALO) + 32)
+    hit = ((n_lane & 63) == from_lane) & ((to_lane < HALO) | (to_lane >= 128 - HALO))
+    place = jnp.where(hit, 1.0, 0.0).astype(BF16)
+
     wait_recv_all(fine_copy, ALONG)
-    waves(ext, forc, r1, s_out, curv, u_out, v_out, planes, 2)
+    own_waves()
     coarse_mid = dot(row_means(planes, 0, 3, 2, 1.0 / (16.0 * STEPS)), pool_mid)
 
-    rows = slice(TOP - 8, TOP + TR + 8)
-    halo_lane = iota((TR + 16, 128), 1)
-    for f in range(5):
-        left = pltpu.roll(ext[f, rows, 0:128], HALO, 1)
-        right = pltpu.roll(ext[f, rows, 128:256], 128 - HALO, 1)
-        e_ext[f, rows, :] = jnp.where(halo_lane < EC // 2, left, right)
-
-    wait_recv_all(fine_copy, DIRS[:6])
-
+    fill_edge(TOP - 8, 8)
+    fill_edge(TOP + TR, 8)
     def open_corner(t):
         rows = jnp.zeros((8, 128), F32)
         for side in range(2):
             block = jnp.concatenate([
                 jnp.broadcast_to(corner[t, side, 0:1], (4, 128)),
                 jnp.broadcast_to(corner[t, side, 1:2], (4, 128))], axis=0)
-            block = slant(pltpu.roll(block, 32, 1) if side else block, 96)
+            block = slant(block, 96)
             rows = jnp.where(lax.shift_right_logical(lane[0:8], 5) == side, block, rows)
         return rows
 
-    halo = jnp.concatenate([open_corner(0), got[...].T, open_corner(1)], axis=0)
+    wait_recv_all(fine_copy, CROSS)
+    arrived = got[0:64]
+    high = arrived.astype(BF16)
+    rest = arrived - high.astype(F32)
+    middle = rest.astype(BF16)
+    low = (rest - middle.astype(F32)).astype(BF16)
+    moved = lax.dot_general(
+        jnp.concatenate([high, middle, low], axis=0), place,
+        (((0,), (0,)), ((), ())), preferred_element_type=F32)
+    rows = slice(TOP, TOP + TR)
     for f in range(5):
-        left = pltpu.roll(halo, (128 - HALO * f) % 128, 1)
-        right = pltpu.roll(halo, 128 - HALO - 32 - HALO * f, 1)
-        e_ext[f, rows, :] = jnp.where(
-            halo_lane < HALO, left, jnp.where(halo_lane >= 128 - HALO, right, e_ext[f, rows, :]))
-    waves(e_ext, e_forc, e_r1, e_s, e_curv, e_u, e_v, e_planes, 1)
+        e_ext[f, rows, :] = e_ext[f, rows, :] + moved[:, 128 * f:128 * f + 128]
+    wait_recv_all(fine_copy, DIRS[2:6])
+    few = iota((8, 128), 1)
+    for t in range(2):
+        halo = open_corner(t)
+        at = TOP - 8 if t == 0 else TOP + TR
+        for f in range(5):
+            left = pltpu.roll(halo, (128 - HALO * f) % 128, 1)
+            right = pltpu.roll(halo, 128 - HALO - 32 - HALO * f, 1)
+            e_ext[f, at:at + 8, :] = jnp.where(
+                few < HALO, left, jnp.where(few >= 128 - HALO, right, e_ext[f, at:at + 8, :]))
+    edge_waves()
 
     means = row_means(e_planes, 0, 3, 1, 1.0 / (16.0 * STEPS))
     edges = dot_nt(edge_side, means)
     ts_s[0] = edges[0:8]
     ts_s[1] = edges[8:16]
     start_all(copy_s, CROSS)
-    coarse = dot(means, pool_side)
+    coarse = dot(means, pool_corner)
     small = iota((8, 128), 1)
+    group = lax.shift_right_logical(small, 3)
+    row = iota((8, 128), 0)
     for t in range(2):
         for side in range(2):
-            at = 0 if side else CC - 8
             packed = [jnp.zeros((8, 128), F32)] * 2
             for f in range(3):
                 r = f * CR + (0 if t == 0 else CR - 8)
-                block = jnp.where((small >= at) & (small < at + 8), coarse[r:r + 8], 0.0)
-                block = pltpu.roll(block, (128 - at + 64 * (f % 2)) % 128, 1, stride=8, stride_axis=0)
-                packed[f // 2] = packed[f // 2] + block
+                block = coarse[r:r + 8, 128 * side:128 * side + 128]
+                packed[f // 2] = packed[f // 2] + jnp.where(group == row + 8 * (f % 2), block, 0.0)
             for k in range(2):
                 corner_s_send[t, side, k:k + 1] = jnp.sum(packed[k], axis=0, keepdims=True)
     start_all(copy_s, DIRS[2:6])
-    coarse = coarse + coarse_mid
+    coarse = dot(means, pool_side) + coarse_mid
     for f in range(3):
         cs[f, 8:8 + CR] = coarse[f * CR:(f + 1) * CR]
     start_all(copy_s, ALONG)
@@ -419,6 +503,11 @@
     for ref, edge in ((s_out, e_s), (u_out, e_u), (v_out, e_v)):
         ref[rows, 0:128] = jnp.where(lane < 16, pltpu.roll(edge[rows], 128 - HALO, 1), ref[rows, 0:128])
         ref[rows, 128:256] = jnp.where(lane >= 112, pltpu.roll(edge[rows], HALO, 1), ref[rows, 128:256])
+
+    weights = spread(TC, 128, 1, (128, TC), 0, True)
+    cols_out[...] = jnp.concatenate([weights, weights], axis=0)
+    weights = spread(TR, WR, 0, (TR, WR), 8, False)
+    rows_out[...] = jnp.concatenate([weights, weights], axis=1)
 
     wait_recv_all(copy_w, CROSS)
     mid = side_w[...].T
@@ -430,21 +519,27 @@
     inside = depth > 0.25
     inv_depth = 1.0 / jnp.maximum(depth, 0.25)
 
-    wait_recv_all(copy_s)
+    wait_send_all(fine_copy)
+    wait_send_all(copy_w, CROSS)
+
+    wait_recv_all(copy_s, CROSS + ALONG)
     mid = side_s[...].T
+    wait_recv_all(copy_s, DIRS[2:6])
+    blocks = []
+    for t in range(2):
+        for f in range(3):
+            parts = []
+            for side in range(2):
+                block = jnp.broadcast_to(corner_s[t, side, f // 2:f // 2 + 1], (8, 128))
+                parts += list(halves(jnp.where(group == row + 8 * (f % 2), block, 0.0)))
+            blocks.append(jnp.concatenate([x.astype(F32) for x in parts], axis=1))
+    ends = dot(jnp.concatenate(blocks, axis=0).astype(BF16), open_corners)
     wide = []
     for f in range(3):
-        ends = []
-        for t in range(2):
-            rows = cs[f, 0:8] if t == 0 else cs[f, WR - 8:WR]
-            for side in range(2):
-                at = CC if side else 120
-                block = jnp.broadcast_to(corner_s[t, side, f // 2:f // 2 + 1], (8, 128))
-                block = slant(pltpu.roll(block, (at - 64 * (f % 2)) % 128, 1), 120)
-                rows = rows + jnp.where((small >= at) & (small < at + 8), block, 0.0)
-            ends.append(rows)
-        wide.append(jnp.concatenate(
-            [ends[0], cs[f, 8:8 + CR] + mid[f * CR:(f + 1) * CR], ends[1]], axis=0))
+        wide.append(jnp.concatenate([
+            cs[f, 0:8] + ends[8 * f:8 * f + 8],
+            cs[f, 8:8 + CR] + mid[f * CR:(f + 1) * CR],
+            cs[f, WR - 8:WR] + ends[24 + 8 * f:32 + 8 * f]], axis=0))
     s0, s1, s2 = wide
 
     def dr(x):
@@ -473,36 +568,27 @@
 
     flow_out[0] = flow_a
     flow_out[1] = flow_c
-    wait_send_all(fine_copy)
-    wait_send_all(copy_w, CROSS + ALONG)
+    wait_send_all(copy_w, ALONG)
     wait_send_all(copy_s)
 
 
-def finish(s_ref, u_ref, v_ref, flow_ref, mask_ref, s_out, u_out, v_out, ca_out, cc_out, cur, store_sem):
+def finish(s_ref, u_ref, v_ref, flow_ref, mask_ref, cols_ref, rows_ref, s_out, u_out, v_out, ca_out, cc_out, cur, store_sem):
     stores = [
         pltpu.make_async_copy(ref.at[TOP:TOP + TR, 0:TC], out, store_sem.at[k])
         for k, (ref, out) in enumerate(((s_ref, s_out), (u_ref, u_out), (v_ref, v_out)))
     ]
     for cp in stores:
         cp.start()
-    cols_out = spread(TC, 128, 1, (128, TC), 0, True)
-    cols_out = jnp.concatenate([cols_out, cols_out], axis=0)
-    rows_out = spread(TR, WR, 0, (TR, WR), 8, False)
-    rows_out = jnp.concatenate([rows_out, rows_out], axis=1)
     high, low = halves(flow_ref[...].reshape(2 * WR, 128))
-    wide = dot(jnp.concatenate([high, low], axis=1), cols_out)
+    wide = dot(jnp.concatenate([high, low], axis=1), cols_ref[...])
     high, low = halves(jnp.concatenate([wide[0:WR], wide[WR:2 * WR]], axis=1))
-    fine = dot(rows_out, jnp.concatenate([high, low], axis=0))
+    fine = dot(rows_ref[...], jnp.concatenate([high, low], axis=0))
     mask = mask_ref[...]
-    cur[0] = fine[:, 0:TC] * mask
-    cur[1] = fine[:, TC:2 * TC] * mask
-    last = [
-        pltpu.make_async_copy(cur.at[0], ca_out, store_sem.at[3]),
-        pltpu.make_async_copy(cur.at[1], cc_out, store_sem.at[4]),
-    ]
-    for cp in last:
-        cp.start()
-    for cp in stores + last:
+    for k, out in enumerate((ca_out, cc_out)):
+        cur[k] = fine[:, k * TC:k * TC + TC] * mask
+        stores.append(pltpu.make_async_copy(cur.at[k], out, store_sem.at[3 + k]))
+        stores[-1].start()
+    for cp in stores:
         cp.wait()
 
 
@@ -518,9 +604,10 @@
         ships = ship_pressure.shape[0]
         state = pl.pallas_call(
             functools.partial(kernel, mesh_rows, mesh_cols),
-            out_shape=[shape(ER, TC)] * 3 + [shape(2, WR, 128), shape(TR, TC)],
+            out_shape=[shape(ER, TC)] * 3 + [shape(2, WR, 128), shape(TR, TC)] + [
+                jax.ShapeDtypeStruct((256, TC), BF16), jax.ShapeDtypeStruct((TR, 2 * WR), BF16)],
             in_specs=[hbm] * 7,
-            out_specs=[vmem] * 5,
+            out_specs=[vmem] * 7,
             scratch_shapes=[
                 pltpu.VMEM((5, ER, TC), F32),
                 pltpu.VMEM((TR, TC), jnp.int32),
@@ -529,10 +616,11 @@
                 pltpu.VMEM((STEPS, ER, TC), F32),
                 pltpu.VMEM((ER, TC), F32),
                 pltpu.VMEM((ER, TC), F32),
+                pltpu.VMEM((2, ER, TC), F32),
                 pltpu.VMEM((10, TR, 128), F32),
                 pltpu.VMEM((5, ER, EC), F32),
                 pltpu.VMEM((STEPS, ER, EC), F32),
-            ] + [pltpu.VMEM((ER, EC), F32)] * 5 + [
+            ] + [pltpu.VMEM((ER, EC), F32)] * 7 + [
                 pltpu.VMEM((3, TR, 128), F32),
                 pltpu.VMEM((128, 128), F32),
                 pltpu.VMEM((128, 128), F32),
@@ -553,7 +641,7 @@
         return pl.pallas_call(
             finish,
             out_shape=[shape(TR, TC)] * 5,
-            in_specs=[vmem] * 5,
+            in_specs=[vmem] * 7,
             out_specs=[hbm] * 5,
             scratch_shapes=[pltpu.VMEM((2, TR, TC), F32), pltpu.SemaphoreType.DMA((5,))],
             compiler_params=pltpu.CompilerParams(vmem_limit_bytes=16 * 1024 * 1024),

time: 28.8 us -> 28.3 us (0.983)
  the two profiles are of different devices: /device:TPU:8 before, /device:TPU:15 now
where the time goes in v4:
time: 28.3 us; the launch traced here: 28.1 us
  Pallas kernels  27.5 us (97%)
  between operations  0.64 us (2%)
    pallas_call x1, Pallas kernels, per_device(): pl.pallas_call(functools.partial(kernel, mesh_rows, mesh_cols), out_shape...  26.4 us
    pallas_call x1, Pallas kernels, per_device(): pl.pallas_call(finish, out_shape=[shape(TR, TC)] * 5, in_specs=[vmem] * 7...  1.06 us

profile of v4, /device:TPU:15, one launch (start us, length us, event | category | flops | bytes accessed | tf_op | source)
XLA Modules:
  0.0 28.1 jit_solution(11540604200507452713)
XLA Ops:
  0.6 26.4 %shard_map.110 = (f32[160,256]{1,0:T(8,128)S(1)}, f32[160,256]{1,0:T(8,128)S(1)}, f32[160,256]{1,0:T(8,128)S(1)}, f32[2,48,128]{2,1,0:T(8,128)S(1)}, f32[128,256...) custom-call(f32[128,256]{1,0:T(8,128)} %s_in.1, f32[128,256]{1,0:T(8,128)} %u_in.1, ...), custom_call_target="tpu_custom_call" | custom-call | tf_op jit(solution)/shard_map/pallas_call | solution.py:605
  27.1 1.1 %shard_map.111 = (f32[128,256]{1,0:T(8,128)}, f32[128,256]{1,0:T(8,128)}, f32[128,256]{1,0:T(8,128)}, f32[128,256]{1,0:T(8,128)}, f32[128,256]{1,0:T(8,128)}) custom-call(f32[160,256]{1,0:T(8,128)S(1)} %get-tuple-element.12.s_ref, f32[160,256]{1,0:T(8,128)S(1)} %get-tuple-element.13.u_ref, f32[160,256]{1,0:T(8,128)S(1)} %get-tuple-element.14.v_ref, ...), custom_call_target="tpu_custom_call" | custom-call | tf_op jit(solution)/shard_map/pallas_call | solution.py:641

commit v5 on v4

--- a/solution.py
+++ b/solution.py
@@ -37,6 +37,8 @@
 ALONG = [(-1, 0), (1, 0)]
 DIRS = CROSS + [(-1, -1), (-1, 1), (1, -1), (1, 1)] + ALONG
 HALO = 6
+SENT = (5, 5, 5, 3, 5)
+FIRST = (0, 5, 10, 20, 15)
 E_BOTH = [(TOP - 8, TR // 2 + 8), (TOP + TR // 2, TR // 2 + 8)]
 E_OWN = [(TOP, TR // 2), (TOP + TR // 2, TR // 2)]
 E_ALL = [(TOP - 8, 8)] + E_OWN + [(TOP + TR, 8)]
@@ -122,7 +124,7 @@
         return (a + da, c + dc)
 
     barrier = pltpu.get_barrier_semaphore()
-    for da, dc in DIRS:
+    for da, dc in DIRS[2:6] + CROSS + ALONG:
         @pl.when(there(da, dc))
         def _(da=da, dc=dc):
             pl.semaphore_signal(barrier, inc=1, device_id=device(da, dc), device_id_type=MESH)
@@ -143,6 +145,8 @@
     for ref in (r1, s_out, u_out, v_out, curv, e_r1, e_s, e_u, e_v, e_curv):
         ref[0:8, :] = jnp.zeros((8, ref.shape[1]), F32)
         ref[ER - 8:ER, :] = jnp.zeros((8, ref.shape[1]), F32)
+    for k in range(2):
+        got[32 * k + 24:32 * k + 32] = jnp.zeros((8, 128), F32)
     for side in (side_w, side_s):
         side[0:CC] = jnp.zeros((CC, 128), F32)
         side[CC + 8:120] = jnp.zeros((112 - CC, 128), F32)
@@ -160,7 +164,7 @@
                 return
             right = 1 if dc > 0 else 0
             if da == 0:
-                got[32 * right:32 * right + 32] = jnp.zeros((32, 128), F32)
+                got[32 * right:32 * right + 24] = jnp.zeros((24, 128), F32)
                 at = CC if right else 120
                 side_w[at:at + 8] = jnp.zeros((8, 128), F32)
                 side_s[at:at + 8] = jnp.zeros((8, 128), F32)
@@ -178,10 +182,23 @@
 
     lane = iota((TR, 128), 1)
     packed = jnp.zeros((TR, 128), F32)
-    for f in range(5):
-        for part, start, move in ((1, HALO * f, HALO * f + HALO), (0, 32 + HALO * f, 32 + HALO * f)):
-            edge = pltpu.roll(ext[f, TOP:TOP + TR, 128 * part:128 * part + 128], move, 1)
-            packed = jnp.where((lane >= start) & (lane < start + HALO), edge, packed)
+    for part in range(2):
+        surface, along, cross, depth, wet = (
+            ext[f, TOP:TOP + TR, 128 * part:128 * part + 128] for f in range(5))
+        far = 128 - lane if part else lane + 1
+        product = (far == 4) | (far == 5)
+        flow = depth * cross
+        beyond = -col_prev(flow) if part else col_next(flow)
+        edges = (
+            jnp.where(far == 5, surface - (0.5 * CONTINUITY) * beyond, surface),
+            jnp.where(product, depth * along, along),
+            jnp.where(product, flow, cross),
+            depth, wet)
+        for f in range(5):
+            start = FIRST[f] + (0 if part else 32)
+            move = start + (SENT[f] if part else 0)
+            packed = jnp.where(
+                (lane >= start) & (lane < start + SENT[f]), pltpu.roll(edges[f], move, 1), packed)
     packt[...] = packed.T
     for t in range(2):
         rows = packed[0:8] if t == 0 else packed[TR - 8:TR]
@@ -195,7 +212,7 @@
         da, dc = DIRS[n]
         if da == 0:
             at = 0 if dc > 0 else 32
-            src, dst = packt.at[at:at + 32], got.at[at:at + 32]
+            src, dst = packt.at[at:at + 24], got.at[at:at + 24]
         elif dc == 0:
             src = ext.at[:, TOP:TOP + 8, 0:TC] if da < 0 else ext.at[:, TOP + TR - 8:TOP + TR, 0:TC]
             dst = ext.at[:, TOP + TR:TOP + TR + 8, 0:TC] if da < 0 else ext.at[:, TOP - 8:TOP, 0:TC]
@@ -424,15 +441,22 @@
             left = pltpu.roll(ext[f, r:r + n, 0:128], HALO, 1)
             right = pltpu.roll(ext[f, r:r + n, 128:256], 128 - HALO, 1)
             both = jnp.where(at < EC // 2, left, right)
-            e_ext[f, r:r + n, :] = jnp.where((at >= HALO) & (at < 128 - HALO), both, 0.0)
+            rest = 0.0
+            if f == 3:
+                rest = jnp.where((at < HALO - SENT[f]) | (at >= 128 - HALO + SENT[f]), 1.0, 0.0)
+            e_ext[f, r:r + n, :] = jnp.where((at >= HALO) & (at < 128 - HALO), both, rest)
 
     fill_edge(TOP, TR)
 
     n_lane = iota((192, 5 * 128), 0)
     to = iota((192, 5 * 128), 1)
     to_field, to_lane = lax.shift_right_logical(to, 7), to & 127
-    from_lane = HALO * to_field + jnp.where(to_lane < HALO, to_lane, to_lane - (128 - HALO) + 32)
-    hit = ((n_lane & 63) == from_lane) & ((to_lane < HALO) | (to_lane >= 128 - HALO))
+    hit = jnp.zeros((192, 5 * 128), jnp.bool_)
+    for f in range(5):
+        left = (to_lane >= HALO - SENT[f]) & (to_lane < HALO) & ((n_lane & 63) == to_lane - (HALO - SENT[f]) + FIRST[f])
+        right = (to_lane >= 128 - HALO) & (to_lane < 128 - HALO + SENT[f]) & (
+            (n_lane & 63) == to_lane - (128 - HALO) + 32 + FIRST[f])
+        hit = hit | ((to_field == f) & (left | right))
     place = jnp.where(hit, 1.0, 0.0).astype(BF16)
 
     wait_recv_all(fine_copy, ALONG)
@@ -469,10 +493,11 @@
         halo = open_corner(t)
         at = TOP - 8 if t == 0 else TOP + TR
         for f in range(5):
-            left = pltpu.roll(halo, (128 - HALO * f) % 128, 1)
-            right = pltpu.roll(halo, 128 - HALO - 32 - HALO * f, 1)
+            left = pltpu.roll(halo, (HALO - SENT[f] - FIRST[f]) % 128, 1)
+            right = pltpu.roll(halo, 128 - HALO - 32 - FIRST[f], 1)
             e_ext[f, at:at + 8, :] = jnp.where(
-                few < HALO, left, jnp.where(few >= 128 - HALO, right, e_ext[f, at:at + 8, :]))
+                (few >= HALO - SENT[f]) & (few < HALO), left,
+                jnp.where((few >= 128 - HALO) & (few < 128 - HALO + SENT[f]), right, e_ext[f, at:at + 8, :]))
     edge_waves()
 
     means = row_means(e_planes, 0, 3, 1, 1.0 / (16.0 * STEPS))

time: 28.3 us -> 28.2 us (level)
  no operation moved by 1% of the time
where the time goes in v5:
time: 28.2 us; the launch traced here: 28.1 us
  Pallas kernels  27.4 us (97%)
  between operations  0.64 us (2%)
    pallas_call x1, Pallas kernels, per_device(): pl.pallas_call(functools.partial(kernel, mesh_rows, mesh_cols), out_shape...  26.4 us
    pallas_call x1, Pallas kernels, per_device(): pl.pallas_call(finish, out_shape=[shape(TR, TC)] * 5, in_specs=[vmem] * 7...  1.06 us

profile of v5, /device:TPU:15, one launch (start us, length us, event | category | flops | bytes accessed | tf_op | source)
XLA Modules:
  0.0 28.1 jit_solution(7952556648931564987)
XLA Ops:
  0.6 26.4 %shard_map.110 = (f32[160,256]{1,0:T(8,128)S(1)}, f32[160,256]{1,0:T(8,128)S(1)}, f32[160,256]{1,0:T(8,128)S(1)}, f32[2,48,128]{2,1,0:T(8,128)S(1)}, f32[128,256...) custom-call(f32[128,256]{1,0:T(8,128)} %s_in.1, f32[128,256]{1,0:T(8,128)} %u_in.1, ...), custom_call_target="tpu_custom_call" | custom-call | tf_op jit(solution)/shard_map/pallas_call | solution.py:630
  27.0 1.1 %shard_map.111 = (f32[128,256]{1,0:T(8,128)}, f32[128,256]{1,0:T(8,128)}, f32[128,256]{1,0:T(8,128)}, f32[128,256]{1,0:T(8,128)}, f32[128,256]{1,0:T(8,128)}) custom-call(f32[160,256]{1,0:T(8,128)S(1)} %get-tuple-element.12.s_ref, f32[160,256]{1,0:T(8,128)S(1)} %get-tuple-element.13.u_ref, f32[160,256]{1,0:T(8,128)S(1)} %get-tuple-element.14.v_ref, ...), custom_call_target="tpu_custom_call" | custom-call | tf_op jit(solution)/shard_map/pallas_call | solution.py:666

commit v6 on v5

--- a/solution.py
+++ b/solution.py
@@ -75,14 +75,6 @@
 
 def col_prev(x):
     return pltpu.roll(x, 1, 1)
-
-
-def slant(x, step):
-    row = iota(x.shape, 0)
-    for bit in (1, 2, 4):
-        if step * bit % 128:
-            x = jnp.where((row & bit) != 0, pltpu.roll(x, step * bit % 128, 1), x)
-    return x
 
 
 def spread(fine, coarse, fine_dim, shape, first, wrap):
@@ -169,8 +161,8 @@
                 side_w[at:at + 8] = jnp.zeros((8, 128), F32)
                 side_s[at:at + 8] = jnp.zeros((8, 128), F32)
             else:
-                corner[0 if da < 0 else 1, right] = jnp.zeros((2, 128), F32)
-                corner_s[0 if da < 0 else 1, right] = jnp.zeros((2, 128), F32)
+                corner[0 if da < 0 else 1, right] = jnp.zeros((8, 128), F32)
+                corner_s[0 if da < 0 else 1, right] = jnp.zeros((8, 128), F32)
 
     rows_near = 1 + jnp.where(a > 0, 1, 0) + jnp.where(a < mesh_rows - 1, 1, 0)
     cols_near = 1 + jnp.where(c > 0, 1, 0) + jnp.where(c < mesh_cols - 1, 1, 0)
@@ -200,13 +192,8 @@
             packed = jnp.where(
                 (lane >= start) & (lane < start + SENT[f]), pltpu.roll(edges[f], move, 1), packed)
     packt[...] = packed.T
-    for t in range(2):
-        rows = packed[0:8] if t == 0 else packed[TR - 8:TR]
-        for side in range(2):
-            block = jnp.where(lax.shift_right_logical(lane[0:8], 5) == side, rows, 0.0)
-            block = slant(block, 32)
-            corner_send[t, side, 0:1] = jnp.sum(block[0:4], axis=0, keepdims=True)
-            corner_send[t, side, 1:2] = jnp.sum(block[4:8], axis=0, keepdims=True)
+    corner_send[0] = packed[0:8]
+    corner_send[1] = packed[TR - 8:TR]
 
     def fine_copy(n):
         da, dc = DIRS[n]
@@ -218,7 +205,7 @@
             dst = ext.at[:, TOP + TR:TOP + TR + 8, 0:TC] if da < 0 else ext.at[:, TOP - 8:TOP, 0:TC]
         else:
             side = 0 if dc > 0 else 1
-            src = corner_send.at[0 if da < 0 else 1, side]
+            src = corner_send.at[0 if da < 0 else 1]
             dst = corner.at[1 if da < 0 else 0, side]
         return pltpu.make_async_remote_copy(
             src_ref=src, dst_ref=dst, send_sem=f_send.at[n], recv_sem=f_recv.at[n],
@@ -427,14 +414,6 @@
 
     pool_corner = jnp.concatenate([corner_matrix(0), corner_matrix(1)], axis=1)
 
-    def open_matrix(at):
-        lane_of = iota((128, 128), 0)
-        to = iota((128, 128), 1)
-        one = jnp.where((to >= at) & (to < at + 8) & ((lane_of & 7) == to - at), 1.0, 0.0).astype(BF16)
-        return jnp.concatenate([one, one], axis=0)
-
-    open_corners = jnp.concatenate([open_matrix(120), open_matrix(CC)], axis=0)
-
     def fill_edge(r, n):
         at = iota((n, 128), 1)
         for f in range(5):
@@ -465,16 +444,6 @@
 
     fill_edge(TOP - 8, 8)
     fill_edge(TOP + TR, 8)
-    def open_corner(t):
-        rows = jnp.zeros((8, 128), F32)
-        for side in range(2):
-            block = jnp.concatenate([
-                jnp.broadcast_to(corner[t, side, 0:1], (4, 128)),
-                jnp.broadcast_to(corner[t, side, 1:2], (4, 128))], axis=0)
-            block = slant(block, 96)
-            rows = jnp.where(lax.shift_right_logical(lane[0:8], 5) == side, block, rows)
-        return rows
-
     wait_recv_all(fine_copy, CROSS)
     arrived = got[0:64]
     high = arrived.astype(BF16)
@@ -490,7 +459,7 @@
     wait_recv_all(fine_copy, DIRS[2:6])
     few = iota((8, 128), 1)
     for t in range(2):
-        halo = open_corner(t)
+        halo = jnp.where(few < 32, corner[t, 0], corner[t, 1])
         at = TOP - 8 if t == 0 else TOP + TR
         for f in range(5):
             left = pltpu.roll(halo, (HALO - SENT[f] - FIRST[f]) % 128, 1)
@@ -508,16 +477,13 @@
     coarse = dot(means, pool_corner)
     small = iota((8, 128), 1)
     group = lax.shift_right_logical(small, 3)
-    row = iota((8, 128), 0)
     for t in range(2):
         for side in range(2):
-            packed = [jnp.zeros((8, 128), F32)] * 2
+            tile = jnp.zeros((8, 128), F32)
             for f in range(3):
                 r = f * CR + (0 if t == 0 else CR - 8)
-                block = coarse[r:r + 8, 128 * side:128 * side + 128]
-                packed[f // 2] = packed[f // 2] + jnp.where(group == row + 8 * (f % 2), block, 0.0)
-            for k in range(2):
-                corner_s_send[t, side, k:k + 1] = jnp.sum(packed[k], axis=0, keepdims=True)
+                tile = jnp.where(group == f, coarse[r:r + 8, 128 * side:128 * side + 128], tile)
+            corner_s_send[t, side] = tile
     start_all(copy_s, DIRS[2:6])
     coarse = dot(means, pool_side) + coarse_mid
     for f in range(3):
@@ -550,21 +516,21 @@
     wait_recv_all(copy_s, CROSS + ALONG)
     mid = side_s[...].T
     wait_recv_all(copy_s, DIRS[2:6])
-    blocks = []
+    ends = []
     for t in range(2):
         for f in range(3):
-            parts = []
+            block = jnp.zeros((8, 128), F32)
             for side in range(2):
-                block = jnp.broadcast_to(corner_s[t, side, f // 2:f // 2 + 1], (8, 128))
-                parts += list(halves(jnp.where(group == row + 8 * (f % 2), block, 0.0)))
-            blocks.append(jnp.concatenate([x.astype(F32) for x in parts], axis=1))
-    ends = dot(jnp.concatenate(blocks, axis=0).astype(BF16), open_corners)
+                at = CC if side else 120
+                moved = pltpu.roll(corner_s[t, side], at - 8 * f, 1)
+                block = jnp.where((small >= at) & (small < at + 8), moved, block)
+            ends.append(block)
     wide = []
     for f in range(3):
         wide.append(jnp.concatenate([
-            cs[f, 0:8] + ends[8 * f:8 * f + 8],
+            cs[f, 0:8] + ends[f],
             cs[f, 8:8 + CR] + mid[f * CR:(f + 1) * CR],
-            cs[f, WR - 8:WR] + ends[24 + 8 * f:32 + 8 * f]], axis=0))
+            cs[f, WR - 8:WR] + ends[3 + f]], axis=0))
     s0, s1, s2 = wide
 
     def dr(x):
@@ -649,7 +615,7 @@
                 pltpu.VMEM((3, TR, 128), F32),
                 pltpu.VMEM((128, 128), F32),
                 pltpu.VMEM((128, 128), F32),
-            ] + [pltpu.VMEM((2, 2, 2, 128), F32)] * 4 + [
+            ] + [pltpu.VMEM((2, 8, 128), F32)] + [pltpu.VMEM((2, 2, 8, 128), F32)] * 3 + [
                 pltpu.VMEM((2, 8, 128), F32),
                 pltpu.VMEM((2, 8, 128), F32),
                 pltpu.VMEM((128, 128), F32),

time: 28.2 us -> 28.1 us (level)
  no operation moved by 1% of the time
where the time goes in v6:
time: 28.1 us; the launch traced here: 28 us
  Pallas kernels  27.4 us (98%)
  between operations  0.64 us (2%)
    pallas_call x1, Pallas kernels, per_device(): pl.pallas_call(functools.partial(kernel, mesh_rows, mesh_cols), out_shape...  26.3 us
    pallas_call x1, Pallas kernels, per_device(): pl.pallas_call(finish, out_shape=[shape(TR, TC)] * 5, in_specs=[vmem] * 7...  1.06 us

profile of v6, /device:TPU:15, one launch (start us, length us, event | category | flops | bytes accessed | tf_op | source)
XLA Modules:
  0.0 28.0 jit_solution(2844439478873208254)
XLA Ops:
  0.6 26.3 %shard_map.110 = (f32[160,256]{1,0:T(8,128)S(1)}, f32[160,256]{1,0:T(8,128)S(1)}, f32[160,256]{1,0:T(8,128)S(1)}, f32[2,48,128]{2,1,0:T(8,128)S(1)}, f32[128,256...) custom-call(f32[128,256]{1,0:T(8,128)} %s_in.1, f32[128,256]{1,0:T(8,128)} %u_in.1, ...), custom_call_target="tpu_custom_call" | custom-call | tf_op jit(solution)/shard_map/pallas_call | solution.py:596
  26.9 1.1 %shard_map.111 = (f32[128,256]{1,0:T(8,128)}, f32[128,256]{1,0:T(8,128)}, f32[128,256]{1,0:T(8,128)}, f32[128,256]{1,0:T(8,128)}, f32[128,256]{1,0:T(8,128)}) custom-call(f32[160,256]{1,0:T(8,128)S(1)} %get-tuple-element.12.s_ref, f32[160,256]{1,0:T(8,128)S(1)} %get-tuple-element.13.u_ref, f32[160,256]{1,0:T(8,128)S(1)} %get-tuple-element.14.v_ref, ...), custom_call_target="tpu_custom_call" | custom-call | tf_op jit(solution)/shard_map/pallas_call | solution.py:632

commit v7 on v6

--- a/solution.py
+++ b/solution.py
@@ -509,6 +509,10 @@
     depth, wet = cw[0], cw[1]
     inside = depth > 0.25
     inv_depth = 1.0 / jnp.maximum(depth, 0.25)
+    drive = (-0.5 * CIRC_FORCE) * wet * inv_depth
+    hold = wet * (1.0 - 4.0 * VISCOSITY - FRICTION * inv_depth)
+    spill = VISCOSITY * wet
+    slope = (0.5 * CIRC_FORCE) * wet
 
     wait_send_all(fine_copy)
     wait_send_all(copy_w, CROSS)
@@ -533,28 +537,25 @@
             cs[f, WR - 8:WR] + ends[3 + f]], axis=0))
     s0, s1, s2 = wide
 
-    def dr(x):
-        return 0.5 * (pltpu.roll(x, WR - 1, 0) - pltpu.roll(x, 1, 0))
-
-    def dc(x):
-        return 0.5 * (col_next(x) - col_prev(x))
-
-    def laplace(x):
-        return pltpu.roll(x, WR - 1, 0) + pltpu.roll(x, 1, 0) + col_next(x) + col_prev(x) - 4.0 * x
-
-    force_a = -(dr(s0) + dc(s1)) * inv_depth
-    force_c = -(dr(s1) + dc(s2)) * inv_depth
-    flow_a = wet * (CIRC_FORCE * force_a)
-    flow_c = wet * (CIRC_FORCE * force_c)
+    def row_step(x):
+        return pltpu.roll(x, WR - 1, 0) - pltpu.roll(x, 1, 0)
+
+    def col_step(x):
+        return col_next(x) - col_prev(x)
+
+    def around(x):
+        return pltpu.roll(x, WR - 1, 0) + pltpu.roll(x, 1, 0) + col_next(x) + col_prev(x)
+
+    push_a = (row_step(s0) + col_step(s1)) * drive
+    push_c = (row_step(s1) + col_step(s2)) * drive
+    flow_a, flow_c = push_a, push_c
     elevation = jnp.zeros_like(depth)
     for _ in range(CIRC - 1):
-        level = elevation - CIRC_LEVEL * (dr(depth * flow_a) + dc(depth * flow_c))
+        level = elevation - (0.5 * CIRC_LEVEL) * (row_step(depth * flow_a) + col_step(depth * flow_c))
         elevation = jnp.where(inside, level, 0.0)
         flow_a, flow_c = (
-            wet * (flow_a + CIRC_FORCE * (force_a - dr(elevation))
-                   - FRICTION * flow_a * inv_depth + VISCOSITY * laplace(flow_a)),
-            wet * (flow_c + CIRC_FORCE * (force_c - dc(elevation))
-                   - FRICTION * flow_c * inv_depth + VISCOSITY * laplace(flow_c)),
+            push_a + hold * flow_a + spill * around(flow_a) - slope * row_step(elevation),
+            push_c + hold * flow_c + spill * around(flow_c) - slope * col_step(elevation),
         )
 
     flow_out[0] = flow_a

time: 28.1 us -> 28.1 us (level)
  no operation moved by 1% of the time
where the time goes in v7:
time: 28.1 us; the launch traced here: 28 us
  Pallas kernels  27.3 us (97%)
  between operations  0.64 us (2%)
    pallas_call x1, Pallas kernels, per_device(): pl.pallas_call(functools.partial(kernel, mesh_rows, mesh_cols), out_shape...  26.3 us
    pallas_call x1, Pallas kernels, per_device(): pl.pallas_call(finish, out_shape=[shape(TR, TC)] * 5, in_specs=[vmem] * 7...  1.06 us

profile of v7, /device:TPU:15, one launch (start us, length us, event | category | flops | bytes accessed | tf_op | source)
XLA Modules:
  0.0 28.0 jit_solution(16205459272429842182)
XLA Ops:
  0.6 26.3 %shard_map.110 = (f32[160,256]{1,0:T(8,128)S(1)}, f32[160,256]{1,0:T(8,128)S(1)}, f32[160,256]{1,0:T(8,128)S(1)}, f32[2,48,128]{2,1,0:T(8,128)S(1)}, f32[128,256...) custom-call(f32[128,256]{1,0:T(8,128)} %s_in.1, f32[128,256]{1,0:T(8,128)} %u_in.1, ...), custom_call_target="tpu_custom_call" | custom-call | tf_op jit(solution)/shard_map/pallas_call | solution.py:597
  26.9 1.1 %shard_map.111 = (f32[128,256]{1,0:T(8,128)}, f32[128,256]{1,0:T(8,128)}, f32[128,256]{1,0:T(8,128)}, f32[128,256]{1,0:T(8,128)}, f32[128,256]{1,0:T(8,128)}) custom-call(f32[160,256]{1,0:T(8,128)S(1)} %get-tuple-element.12.s_ref, f32[160,256]{1,0:T(8,128)S(1)} %get-tuple-element.13.u_ref, f32[160,256]{1,0:T(8,128)S(1)} %get-tuple-element.14.v_ref, ...), custom_call_target="tpu_custom_call" | custom-call | tf_op jit(solution)/shard_map/pallas_call | solution.py:633
